TPU v7x, 512 devices: a whole 4x4x16 slice. The times are simulated.
512 devices in a mesh: dp: 32 (over y_lo, z), seq: 16 (over y_hi, x, core).
Axes of the slice: x: 4, y: 4 (y_hi: 2, y_lo: 2; y = y_hi * 2 + y_lo), z: 16, core: 2. Of those that a mesh axis runs over, the one named last changes fastest.
Arguments:
- hidden: bfloat16 [64, 1024, 8192], P('dp', 'seq'), may hold values from -6 to 6
- queries: bfloat16 [64, 1024, 4096], P('dp', 'seq'), may hold values from -128 to 128
- keys: bfloat16 [64, 1024, 512], P('dp', 'seq'), may hold values from -8 to 8
- upstream: bfloat16 [64, 1024, 4096], P('dp', 'seq'), may hold values from -6 to 6
- w_value: bfloat16 [8192, 512], P(('dp', 'seq')), may hold values from -0.0625 to 0.0625
- segment_ids: int32 [64, 1024], P('dp', 'seq'), may hold values from 0 to 1, as said below
- response_lengths: int32 [64, 2], P('dp'), may hold values from 1 to 256
- advantages: bfloat16 [64, 2], P('dp'), may hold values from -4 to 4
- move_plan: int32 [32, 2], replicated, may hold values from -1 to 1, as said below
Outputs:
- key_grads: bfloat16 [64, 1024, 512], P('dp', 'seq')
- weight_grads: float32 [8192, 512], P(('dp', 'seq'))
Inputs may be any that keep to these rules, and one draw needn't show every extreme that they name: At section b data rank r trades slot move_plan[r, b] with rank r XOR 2^b, which trades its slot move_plan[r XOR 2^b, b]; the two ranks of a pair are both -1 (no trade) or both not. `segment_ids`: in every slot the positions before a cut belong to rollout 0 and the rest to rollout 1; the cut lies between 256 and 768. `response_lengths`: A response never exceeds its rollout.
All inputs are finite; a program needn't handle non-finite values.
Results may differ from a plain program's by a relative error of at most 0.034.
Values may be sent and summed in bfloat16 or wider, within the bound.
A program may use at most 64 MiB of HBM per device.

v0:
```python
import jax
import jax.numpy as jnp
from jax import lax
from jax.sharding import PartitionSpec as P

KVH = 4
HD = 128


def swapped(block, axis, distance):
    count = lax.axis_size(axis)
    route = []
    for low in range(count):
        high = low | 1 << distance
        if high != low and high < count:
            route += [(low, high), (high, low)]
    return lax.ppermute(block, axis, route)


def for_sending(array):

    def short(part):
        return part.astype(jnp.bfloat16) if part.dtype == jnp.float32 else part

    return jax.tree.map(short, array)


def slot_weights(segment_row, lengths, advantage_row):
    length = segment_row.shape[0]
    member = segment_row[:, None] == jnp.arange(advantage_row.shape[0], dtype=jnp.int32)[None, :]
    counts = jnp.sum(member.astype(jnp.int32), 0)
    endings = jnp.cumsum(counts) - 1
    last_pos = jnp.sum(jnp.where(member, endings[None, :], 0), 1)
    resp_tok = jnp.sum(jnp.where(member, lengths[None, :], 0), 1)
    adv_tok = jnp.sum(
        jnp.where(member, advantage_row.astype(jnp.float32)[None, :], jnp.float32(0.0)), 1
    )
    from_end = last_pos - jnp.arange(length, dtype=jnp.int32)
    return jnp.where(from_end < resp_tok, adv_tok, jnp.float32(0.0))


def take_slot(arrays, chosen):
    return tuple(
        (lax.dynamic_index_in_dim(member_arr, chosen, 0, keepdims=False) for member_arr in arrays)
    )


def put_slot(arrays, incoming, chosen, active):
    result = []
    for current, arrived in zip(arrays, incoming):
        landing = (jnp.arange(current.shape[0], dtype=jnp.int32) == chosen) & active
        landing = landing.reshape((current.shape[0],) + (1,) * (current.ndim - 1))
        result.append(jnp.where(landing, arrived[None], current))
    return tuple(result)


def slot_backward(items):
    query_rows, cot_rows, key_values, segment_row = items
    length = query_rows.shape[0]
    positions = jnp.arange(length, dtype=jnp.int32)
    allowed = (segment_row[:, None] == segment_row[None, :]) & (
        positions[None, :] <= positions[:, None]
    )
    keys_head = key_values[:, :HD]
    values_head = key_values[:, HD:]
    inv_root = HD ** (-0.5)
    contract_rows = (((1,), (1,)), ((), ()))
    contract_cols = (((0,), (0,)), ((), ()))
    key_sum = jnp.zeros((length, HD), jnp.float32)
    value_sum = jnp.zeros((length, HD), jnp.float32)
    for head_idx in range(query_rows.shape[1] // HD):
        query_head = query_rows[:, head_idx * HD : (head_idx + 1) * HD]
        cot_head = cot_rows[:, head_idx * HD : (head_idx + 1) * HD]
        scores = (
            lax.dot_general(
                query_head, keys_head, contract_rows, preferred_element_type=jnp.float32
            )
            * inv_root
        )
        scores = jnp.where(allowed, scores, jnp.float32(-1e30))
        highest = jnp.max(scores, 1, keepdims=True)
        weighted = jnp.where(allowed, jnp.exp(scores - highest), jnp.float32(0.0))
        attn_probs = weighted / jnp.sum(weighted, 1, keepdims=True)
        attn_low = attn_probs.astype(jnp.bfloat16)
        grad_probs = lax.dot_general(
            cot_head, values_head, contract_rows, preferred_element_type=jnp.float32
        )
        grad_scores = attn_probs * (grad_probs - jnp.sum(attn_probs * grad_probs, 1, keepdims=True))
        grad_low = grad_scores.astype(jnp.bfloat16)
        value_sum = value_sum + lax.dot_general(
            attn_low, cot_head, contract_cols, preferred_element_type=jnp.float32
        )
        key_sum = (
            key_sum
            + lax.dot_general(
                grad_low, query_head, contract_cols, preferred_element_type=jnp.float32
            )
            * inv_root
        )
    return (key_sum.astype(jnp.bfloat16), value_sum.astype(jnp.bfloat16))


def on_device(
    hidden, queries, keys, upstream, w_value, segment_ids, response_lengths, advantages, move_plan
):
    n_data = lax.axis_size("dp")
    n_seq = lax.axis_size("seq")
    slot_count, slot_dev, feature_width = hidden.shape
    part_width = feature_width // (n_data * n_seq)
    data_rank = lax.axis_index("dp")
    sections = move_plan.shape[1]
    carried = (queries, keys, upstream, advantages, hidden)
    labels = (segment_ids, response_lengths)
    for section_idx in range(sections):
        giving = move_plan[data_rank, section_idx]
        chosen = jnp.maximum(giving, 0)
        active = giving >= 0
        fetched = swapped(take_slot(labels, chosen), "dp", section_idx)
        labels = put_slot(labels, fetched, chosen, active)
        arrived = swapped(for_sending(take_slot(carried, chosen)), "dp", section_idx)
        carried = put_slot(carried, arrived, chosen, active)
    queries, keys, upstream, advantages, last_item = carried
    blocks = last_item.reshape(slot_count, slot_dev, n_data, n_seq, part_width)
    split_rows = lax.all_to_all(blocks, "seq", split_axis=3, concat_axis=1, tiled=True)
    project_flat_rows = split_rows.reshape(slot_count * slot_dev * n_seq, n_data * part_width)
    columns = project_flat_rows
    partial_values = jnp.dot(
        columns,
        lax.all_gather(w_value, "dp", axis=0, tiled=True),
        preferred_element_type=jnp.float32,
    )
    partial_values = partial_values.reshape(slot_count, slot_dev * n_seq, w_value.shape[1])
    summed = lax.psum_scatter(
        partial_values.astype(jnp.bfloat16), "seq", scatter_dimension=1, tiled=True
    )
    segment_rows, length_rows = labels
    segs_full = lax.all_gather(segment_rows, "seq", axis=1, tiled=True)
    weights_full = jax.vmap(slot_weights)(segs_full, length_rows, advantages)
    seq_rank = lax.axis_index("seq")
    token_weight = lax.dynamic_slice_in_dim(weights_full, seq_rank * slot_dev, slot_dev, 1)
    cotangent = (upstream.astype(jnp.float32) * token_weight[:, :, None]).astype(jnp.bfloat16)
    copies = n_seq // KVH
    shape_rep = (slot_count, slot_dev, KVH, copies, HD)
    key_rep = jnp.broadcast_to(keys.reshape(slot_count, slot_dev, KVH, 1, HD), shape_rep)
    value_rep = jnp.broadcast_to(summed.reshape(slot_count, slot_dev, KVH, 1, HD), shape_rep)
    paired = jnp.concatenate([key_rep, value_rep], 4).reshape(slot_count, slot_dev, n_seq * 2 * HD)
    query_heads, cot_heads, kv_heads = (
        lax.all_to_all(queries, "seq", split_axis=2, concat_axis=1, tiled=True),
        lax.all_to_all(cotangent, "seq", split_axis=2, concat_axis=1, tiled=True),
        lax.all_to_all(paired, "seq", split_axis=2, concat_axis=1, tiled=True),
    )
    key_part, value_part = lax.map(slot_backward, (query_heads, cot_heads, kv_heads, segs_full))

    def merge_heads(returned):
        grouped = returned.reshape(slot_count, slot_dev, KVH, copies, HD).astype(jnp.float32)
        return jnp.sum(grouped, 3).astype(jnp.bfloat16).reshape(slot_count, slot_dev, KVH * HD)

    key_back, value_back = (
        lax.all_to_all(key_part, "seq", split_axis=1, concat_axis=2, tiled=True),
        lax.all_to_all(value_part, "seq", split_axis=1, concat_axis=2, tiled=True),
    )
    key_grads = merge_heads(key_back)
    gathered = lax.all_gather(merge_heads(value_back), "seq", axis=1, tiled=True)
    grads_flat = gathered.reshape(slot_count * slot_dev * n_seq, gathered.shape[2])
    columns = project_flat_rows
    weight_out = lax.psum_scatter(
        lax.dot_general(
            columns, grads_flat, (((0,), (0,)), ((), ())), preferred_element_type=jnp.float32
        ).astype(jnp.bfloat16),
        "dp",
        scatter_dimension=0,
        tiled=True,
    ).astype(jnp.float32)
    return (key_grads, weight_out)


def solution(mesh):
    placed = (
        P("dp", "seq", None),
        P("dp", "seq", None),
        P("dp", "seq", None),
        P("dp", "seq", None),
        P(("dp", "seq"), None),
        P("dp", "seq"),
        P("dp", None),
        P("dp", None),
        P(),
    )
    return jax.shard_map(
        on_device,
        mesh=mesh,
        in_specs=placed,
        out_specs=(P("dp", "seq", None), P(("dp", "seq"), None)),
        check_vma=False,
    )
```

profile of v0, /device:TPU:6, one launch (start us, length us, event | category | flops | bytes accessed | tf_op | source)
XLA Modules:
  0.0 671.3 jit_solution(17866464559339517030)
XLA Ops:
  9.9 3.8 collective-permute-start
  17.1 3.8 collective-permute-start.12
  27.1 3.8 collective-permute-start.6
  32.8 96.9 %all_gather.10 = bf16[512,512]{1,0:T(8,128)(2,1)} all-gather(bf16[16,512]{1,0:T(8,128)(2,1)} %param.15), channel_id=1, replica_groups=mesh['dp'=32,'seq'=16] {'dp'}, dimensions={0}, use_global_device_ids=true | all-gather | bytes 540672 | tf_op jit(solution)/shard_map/all_gather | solution.py:129
  135.6 4.8 collective-permute-start.11
  141.9 4.3 collective-permute-done.13
  146.2 5.2 collective-permute-start.7
  153.5 23.4 %collective-permute-done.1 = s32[64]{0:T(128)S(1)} collective-permute-done((s32[64]{0:T(128)S(1)}, s32[64]{0:T(128)S(1)}, u32[]{:S(2)}, u32[]{:S(2)}) %collective-permute-start.1) | collective-permute-done | bytes 288 | tf_op jit(solution)/shard_map/ppermute | solution.py:17
  177.0 18.3 %all-gather = s32[16,64,2]{1,2,0:T(2,128)S(1)} all-gather(s32[1,64,2]{1,2,0:T(2,128)S(1)} %select_bitcast_fusion), channel_id=1, replica_groups=mesh['dp'=32,'seq'=16] {'seq'}, dimensions={0}, use_global_device_ids=true | all-gather | bytes 8704 | tf_op jit(solution)/shard_map/all_gather | solution.py:137
  195.6 2.9 broadcast_select_fusion.1
  198.5 4.8 copy.74
  203.2 5.3 copy.100
  208.6 7.6 %reshape.126 = bf16[16,2,32768]{2,1,0:T(2,128)(2,1)} reshape(bf16[16,2,32,16,64]{4,3,2,1,0:T(8,128)(2,1)} %bitcast.126) | data formatting | bytes 4194304
  216.1 9.7 %all-to-all-start.1 = ((bf16[16,2,32768]{2,1,0:T(2,128)(2,1)}), bf16[16,2,32768]{2,1,0:T(2,128)(2,1)S(1)}, u32[]{:S(2)}, u32[]{:S(2)}) async-start(bf16[16,2,32768]{2,1,0:T(2,128)(2,1)} %reshape.126), calls=%async_computation.1 | async-start | bytes 4194304 | tf_op jit(solution)/shard_map/all_to_all | solution.py:124
  231.8 20.3 %all-to-all-done.1 = bf16[16,2,32768]{2,1,0:T(2,128)(2,1)S(1)} async-done(((bf16[16,2,32768]{2,1,0:T(2,128)(2,1)}), bf16[16,2,32768]{2,1,0:T(2,128)(2,1)S(1)}, u32[]{:S(2)}, u32[]{:S(2)}) %all-to-all-start.1) | async-done | bytes 2097184 | tf_op jit(solution)/shard_map/all_to_all | solution.py:124
  252.1 5.0 reshape.127
  257.1 2.9 bitcast_bitcast_fusion
  262.0 6.8 %copy.76 = bf16[2,16,64,32,1,16]{2,1,5,3,0,4:T(8,128)(2,1)} copy(bf16[2,16,64,32,1,16]{2,5,3,0,1,4:T(8,128)(2,1)S(1)} %bitcast_bitcast_fusion) | data formatting | bytes 4194304 | tf_op jit(solution)/shard_map/all_to_all | solution.py:124
  268.8 6.6 dot_general.32
  275.4 4.3 convolution_convert_fusion
  282.5 2.4 multiply_convert_fusion.14
  284.9 5.1 copy.81
  290.0 2.3 reshape.130
  292.4 7.9 %all-to-all-start.3 = ((bf16[16,2,16384]{2,1,0:T(2,128)(2,1)}), bf16[16,2,16384]{2,1,0:T(2,128)(2,1)}, u32[]{:S(2)}, u32[]{:S(2)}) async-start(bf16[16,2,16384]{2,1,0:T(2,128)(2,1)} %reshape.130), calls=%async_computation.4 | async-start | bytes 2097152 | tf_op jit(solution)/shard_map/all_to_all | solution.py:149
  300.3 3.9 collective-permute-start.4
  304.2 4.2 collective-permute-done.3
  310.7 5.0 copy.71
  318.0 7.6 %all-to-all-start = ((bf16[16,2,16384]{2,1,0:T(2,128)(2,1)}), bf16[16,2,16384]{2,1,0:T(2,128)(2,1)S(1)}, u32[]{:S(2)}, u32[]{:S(2)}) async-start(bf16[16,2,16384]{2,1,0:T(2,128)(2,1)} %reshape.124), calls=%async_computation | async-start | bytes 2097152 | tf_op jit(solution)/shard_map/all_to_all | solution.py:148
  327.9 5.9 collective-permute-done.5
  334.1 38.6 %reduce-scatter.3.cloned.1.call-done = bf16[2,64,512]{2,1,0:T(8,128)(2,1)} async-done(((bf16[2,1024,512]{2,1,0:T(8,128)(2,1)}), bf16[2,64,512]{2,1,0:T(8,128)(2,1)}) %reduce-scatter.3.cloned.1.call-update) | async-done | bytes 131088 | tf_op jit(solution)/shard_map/reduce_scatter | solution.py:133
  375.4 3.2 pad_maximum_fusion
  378.6 2.3 reshape.128
  381.0 5.3 all-to-all-start.2
  386.4 5.0 reshape.131
  392.8 5.7 reshape.125
  398.5 4.6 copy.72
  403.2 5.7 reshape.129
  408.9 4.6 copy.94
  413.5 28.7 %while.12 = (s32[]{:T(128)}, bf16[2,1024,128]{2,1,0:T(8,128)(2,1)}, bf16[2,1024,128]{2,1,0:T(8,128)(2,1)}, s32[2,1024]{1,0:T(2,128)S(1)}, bf16[2,1024,256]{2,1,0...) while((s32[]{:T(128)}, bf16[2,1024,128]{2,1,0:T(8,128)(2,1)}, ...), condition=%wide.region_13.14_spmd, body=%wide.region_6.13_spmd.sunk | while | flops 2234116096 | bytes 76185824 | solution.py:152
  424.8 2.5 fusion.85
  438.9 2.5 fusion.85
  443.8 16.7 %all_to_all.99 = bf16[2,1024,128]{2,0,1:T(2,128)(2,1)S(1)} all-to-all(bf16[2,1024,128]{2,0,1:T(2,128)(2,1)S(1)} %copy.87), channel_id=1, replica_groups=mesh['dp'=32,'seq'=16] {'seq'}, dimensions={1} | all-to-all | bytes 1048576 | tf_op jit(solution)/shard_map/all_to_all | solution.py:160
  462.0 9.0 %copy.86 = bf16[2,16,64,32,1,16]{2,1,0,5,3,4:T(8,128)(2,1)} copy(bf16[2,16,64,32,1,16]{2,5,3,0,1,4:T(8,128)(2,1)} %copy-done) | data formatting | bytes 4194304 | tf_op jit(solution)/shard_map/all_to_all | solution.py:124
  471.1 5.8 reshape.117
  476.8 48.1 %all-gather.3.cloned.1.call-done = bf16[2,1024,512]{2,1,0:T(8,128)(2,1)} async-done(((bf16[2,64,512]{2,1,0:T(8,128)(2,1)}), bf16[2,1024,512]{2,1,0:T(8,128)(2,1)}) %all-gather.3.cloned.1.call-update) | async-done | bytes 2097168 | tf_op jit(solution)/shard_map/all_gather | solution.py:163
  525.0 3.6 convolution_convert_fusion.1
  529.2 13.8 %all_to_all.100 = bf16[2,1024,128]{2,0,1:T(2,128)(2,1)S(1)} all-to-all(bf16[2,1024,128]{2,0,1:T(2,128)(2,1)S(1)} %copy.83), channel_id=1, replica_groups=mesh['dp'=32,'seq'=16] {'seq'}, dimensions={1} | all-to-all | bytes 1048576 | tf_op jit(solution)/shard_map/all_to_all | solution.py:159
  544.5 118.7 %reduce-scatter.5.cloned.1.call-done = bf16[16,512]{1,0:T(8,128)(2,1)} async-done(((bf16[512,512]{1,0:T(8,128)(2,1)}), bf16[16,512]{1,0:T(8,128)(2,1)}) %reduce-scatter.5.cloned.1.call-update) | async-done | bytes 16400 | tf_op jit(solution)/shard_map/reduce_scatter | solution.py:166
  (138 shorter events, 73.0 us)
Async XLA Ops:
  7.2 128.4 %copy-start.12 = (s32[2,2]{1,0:T(2,128)S(1)}, s32[2,2]{1,0:T(2,128)}, u32[]{:S(2)}) copy-start(s32[2,2]{1,0:T(2,128)} %param.17) | copy-start | bytes 52
  7.2 126.3 %copy-start.14 = (bf16[2,2]{1,0:T(2,128)(2,1)S(1)}, bf16[2,2]{1,0:T(2,128)(2,1)}, u32[]{:S(2)}) copy-start(bf16[2,2]{1,0:T(2,128)(2,1)} %param.18) | copy-start | bytes 28
  7.2 133.3 %copy-start.1 = (bf16[2,64,8192]{2,1,0:T(8,128)(2,1)S(1)}, bf16[2,64,8192]{2,1,0:T(8,128)(2,1)}, u32[]{:S(2)}) copy-start(bf16[2,64,8192]{2,1,0:T(8,128)(2,1)} %param.11) | copy-start | bytes 6291460
  9.9 141.5 %collective-permute-start = (s32[64]{0:T(128)S(1)}, s32[64]{0:T(128)S(1)}, u32[]{:S(2)}, u32[]{:S(2)}) collective-permute-start(s32[64]{0:T(128)S(1)} %fusion.55), channel_id=1, source_target_pairs={{0,16},{16,0},{32,48},{48,32},{64,80},{80,64},{96,112},{112,96},{1... | collective-permute-start | bytes 776 | tf_op jit(solution)/shard_map/ppermute | solution.py:17
  14.4 119.2 %collective-permute-start.10 = (s32[2]{0:T(128)S(1)}, s32[2]{0:T(128)S(1)}, u32[]{:S(2)}, u32[]{:S(2)}) collective-permute-start(s32[2]{0:T(128)S(1)} %fusion.57), channel_id=1, source_target_pairs={{0,16},{16,0},{32,48},{48,32},{64,80},{80,64},{96,112},{112,96},{1... | collective-permute-start | bytes 32 | tf_op jit(solution)/shard_map/ppermute | solution.py:17
  17.1 114.5 %collective-permute-start.12 = (bf16[2]{0:T(256)(128)(2,1)S(1)}, bf16[2]{0:T(256)(128)(2,1)S(1)}, u32[]{:S(2)}, u32[]{:S(2)}) collective-permute-start(bf16[2]{0:T(256)(128)(2,1)S(1)} %fusion.59), channel_id=1, source_target_pairs={{0,16},{16,0},{32,48},{48,32},{64,80},{80,64},{96,112},{112,96},{1... | collective-permute-start | bytes 20 | tf_op jit(solution)/shard_map/ppermute | solution.py:17
  22.8 203.6 %collective-permute-start.2 = (bf16[64,4096]{1,0:T(8,128)(2,1)}, bf16[64,4096]{1,0:T(8,128)(2,1)}, u32[]{:S(2)}, u32[]{:S(2)}) collective-permute-start(bf16[64,4096]{1,0:T(8,128)(2,1)} %dynamic-slice_bitcast_fusion.8), channel_id=1, source_target_pairs={{0,16},{16,0},{32,48},{48,32},{64,80},{80,64},{96,112},{112,96},{1... | collective-permute-start | bytes 1572872 | tf_op jit(solution)/shard_map/ppermute | solution.py:17
  27.1 108.5 %collective-permute-start.6 = (bf16[64,8192]{1,0:T(8,128)(2,1)}, bf16[64,8192]{1,0:T(8,128)(2,1)S(1)}, u32[]{:S(2)}, u32[]{:S(2)}) collective-permute-start(bf16[64,8192]{1,0:T(8,128)(2,1)} %dynamic-slice_bitcast_fusion.4), channel_id=1, source_target_pairs={{0,16},{16,0},{32,48},{48,32},{64,80},{80,64},{96,112},{112,96},{1... | collective-permute-start | bytes 3145736 | tf_op jit(solution)/shard_map/ppermute | solution.py:17
  129.7 21.7 %copy-start.13 = (s32[2,64]{1,0:T(2,128)S(1)}, s32[2,64]{1,0:T(2,128)}, u32[]{:S(2)}) copy-start(s32[2,64]{1,0:T(2,128)} %param.16) | copy-start | bytes 1540
  131.6 94.8 %collective-permute-start.8 = (bf16[64,4096]{1,0:T(8,128)(2,1)}, bf16[64,4096]{1,0:T(8,128)(2,1)}, u32[]{:S(2)}, u32[]{:S(2)}) collective-permute-start(bf16[64,4096]{1,0:T(8,128)(2,1)} %dynamic-slice_bitcast_fusion.6), channel_id=1, source_target_pairs={{0,16},{16,0},{32,48},{48,32},{64,80},{80,64},{96,112},{112,96},{1... | collective-permute-start | bytes 1572872 | tf_op jit(solution)/shard_map/ppermute | solution.py:17
  133.6 12.6 %collective-permute-start.13 = (bf16[2]{0:T(256)(128)(2,1)S(1)}, bf16[2]{0:T(256)(128)(2,1)S(1)}, u32[]{:S(2)}, u32[]{:S(2)}) collective-permute-start(bf16[2]{0:T(256)(128)(2,1)S(1)} %fusion.60), channel_id=1, source_target_pairs={{0,32},{32,0},{16,48},{48,16},{64,96},{96,64},{80,112},{112,80},{1... | collective-permute-start | bytes 20 | tf_op jit(solution)/shard_map/ppermute | solution.py:17
  135.6 17.8 %collective-permute-start.11 = (s32[2]{0:T(128)S(1)}, s32[2]{0:T(128)S(1)}, u32[]{:S(2)}, u32[]{:S(2)}) collective-permute-start(s32[2]{0:T(128)S(1)} %fusion.58), channel_id=1, source_target_pairs={{0,32},{32,0},{16,48},{48,16},{64,96},{96,64},{80,112},{112,80},{1... | collective-permute-start | bytes 32 | tf_op jit(solution)/shard_map/ppermute | solution.py:17
  146.2 49.4 %collective-permute-start.7 = (bf16[64,8192]{1,0:T(8,128)(2,1)}, bf16[64,8192]{1,0:T(8,128)(2,1)}, u32[]{:S(2)}, u32[]{:S(2)}) collective-permute-start(bf16[64,8192]{1,0:T(8,128)(2,1)} %dynamic-slice_bitcast_fusion.3), channel_id=1, source_target_pairs={{0,32},{32,0},{16,48},{48,16},{64,96},{96,64},{80,112},{112,80},{1... | collective-permute-start | bytes 3145736 | tf_op jit(solution)/shard_map/ppermute | solution.py:17
  151.5 25.5 %collective-permute-start.1 = (s32[64]{0:T(128)S(1)}, s32[64]{0:T(128)S(1)}, u32[]{:S(2)}, u32[]{:S(2)}) collective-permute-start(s32[64]{0:T(128)S(1)} %fusion.56), channel_id=1, source_target_pairs={{0,32},{32,0},{16,48},{48,16},{64,96},{96,64},{80,112},{112,80},{1... | collective-permute-start | bytes 776 | tf_op jit(solution)/shard_map/ppermute | solution.py:17
  216.1 36.0 %all-to-all-start.1 = ((bf16[16,2,32768]{2,1,0:T(2,128)(2,1)}), bf16[16,2,32768]{2,1,0:T(2,128)(2,1)S(1)}, u32[]{:S(2)}, u32[]{:S(2)}) async-start(bf16[16,2,32768]{2,1,0:T(2,128)(2,1)} %reshape.126), calls=%async_computation.1 | async-start | bytes 4194304 | tf_op jit(solution)/shard_map/all_to_all | solution.py:124
  225.8 146.8 %reduce-scatter.3.cloned.1.call-start = ((), (), s32[]{:S(2)}) async-start(), calls=%async_computation.8 | async-start | bytes 2228224 | tf_op jit(solution)/shard_map/reduce_scatter | solution.py:133
  228.6 1.2 copy-start.2
  229.7 52.8 %collective-permute-start.9 = (bf16[64,4096]{1,0:T(8,128)(2,1)}, bf16[64,4096]{1,0:T(8,128)(2,1)}, u32[]{:S(2)}, u32[]{:S(2)}) collective-permute-start(bf16[64,4096]{1,0:T(8,128)(2,1)} %dynamic-slice_bitcast_fusion.5), channel_id=1, source_target_pairs={{0,32},{32,0},{16,48},{48,16},{64,96},{96,64},{80,112},{112,80},{1... | collective-permute-start | bytes 1572872 | tf_op jit(solution)/shard_map/ppermute | solution.py:17
  260.0 1.9 copy-start
  268.8 6.6 copy-start.6
  275.4 7.1 %copy-start.3 = (bf16[2,64,4096]{2,1,0:T(8,128)(2,1)S(1)}, bf16[2,64,4096]{2,1,0:T(8,128)(2,1)}, u32[]{:S(2)}) copy-start(bf16[2,64,4096]{2,1,0:T(8,128)(2,1)} %copy-done.2) | copy-start | bytes 3145732
  280.6 27.8 %collective-permute-start.3 = (bf16[64,4096]{1,0:T(8,128)(2,1)}, bf16[64,4096]{1,0:T(8,128)(2,1)}, u32[]{:S(2)}, u32[]{:S(2)}) collective-permute-start(bf16[64,4096]{1,0:T(8,128)(2,1)} %dynamic-slice_bitcast_fusion.7), channel_id=1, source_target_pairs={{0,32},{32,0},{16,48},{48,16},{64,96},{96,64},{80,112},{112,80},{1... | collective-permute-start | bytes 1572872 | tf_op jit(solution)/shard_map/ppermute | solution.py:17
  284.9 15.3 %copy-start.5 = (bf16[2,64,512]{2,1,0:T(8,128)(2,1)S(1)}, bf16[2,64,512]{2,1,0:T(8,128)(2,1)}, u32[]{:S(2)}) copy-start(bf16[2,64,512]{2,1,0:T(8,128)(2,1)} %param.13) | copy-start | bytes 393220
  292.4 25.7 %all-to-all-start.3 = ((bf16[16,2,16384]{2,1,0:T(2,128)(2,1)}), bf16[16,2,16384]{2,1,0:T(2,128)(2,1)}, u32[]{:S(2)}, u32[]{:S(2)}) async-start(bf16[16,2,16384]{2,1,0:T(2,128)(2,1)} %reshape.130), calls=%async_computation.4 | async-start | bytes 2097152 | tf_op jit(solution)/shard_map/all_to_all | solution.py:149
  300.3 25.4 %collective-permute-start.4 = (bf16[64,512]{1,0:T(8,128)(2,1)S(1)}, bf16[64,512]{1,0:T(8,128)(2,1)S(1)}, u32[]{:S(2)}, u32[]{:S(2)}) collective-permute-start(bf16[64,512]{1,0:T(8,128)(2,1)S(1)} %dynamic-slice_bitcast_fusion.10), channel_id=1, source_target_pairs={{0,16},{16,0},{32,48},{48,32},{64,80},{80,64},{96,112},{112,96},{1... | collective-permute-start | bytes 196616 | tf_op jit(solution)/shard_map/ppermute | solution.py:17
  318.0 62.9 %all-to-all-start = ((bf16[16,2,16384]{2,1,0:T(2,128)(2,1)}), bf16[16,2,16384]{2,1,0:T(2,128)(2,1)S(1)}, u32[]{:S(2)}, u32[]{:S(2)}) async-start(bf16[16,2,16384]{2,1,0:T(2,128)(2,1)} %reshape.124), calls=%async_computation | async-start | bytes 2097152 | tf_op jit(solution)/shard_map/all_to_all | solution.py:148
  325.7 8.1 %collective-permute-start.5 = (bf16[64,512]{1,0:T(8,128)(2,1)S(1)}, bf16[64,512]{1,0:T(8,128)(2,1)S(1)}, u32[]{:S(2)}, u32[]{:S(2)}) collective-permute-start(bf16[64,512]{1,0:T(8,128)(2,1)S(1)} %dynamic-slice_bitcast_fusion.9), channel_id=1, source_target_pairs={{0,32},{32,0},{16,48},{48,16},{64,96},{96,64},{80,112},{112,80},{1... | collective-permute-start | bytes 196616 | tf_op jit(solution)/shard_map/ppermute | solution.py:17
  380.9 5.4 copy-start.4
  381.0 22.2 %all-to-all-start.2 = ((bf16[16,2,16384]{2,1,0:T(2,128)(2,1)}), bf16[16,2,16384]{2,1,0:T(2,128)(2,1)}, u32[]{:S(2)}, u32[]{:S(2)}) async-start(bf16[16,2,16384]{2,1,0:T(2,128)(2,1)} %reshape.128), calls=%async_computation.3 | async-start | bytes 2097152 | tf_op jit(solution)/shard_map/all_to_all | solution.py:150
  386.3 138.7 %all-gather.3.cloned.1.call-start = ((), (), s32[]{:S(2)}) async-start(), calls=%async_computation.9 | async-start | bytes 2228224 | tf_op jit(solution)/shard_map/all_gather | solution.py:163
  417.6 2.0 copy-start.7
  421.9 1.3 copy-start.8
  423.2 1.5 copy-start.9
  427.2 0.8 copy-start.10
  431.8 2.0 copy-start.7
  436.0 1.3 copy-start.8
  437.4 1.5 copy-start.9
  441.4 0.8 copy-start.10
  462.0 201.2 %reduce-scatter.5.cloned.1.call-start = ((), (), s32[]{:S(2)}) async-start(), calls=%async_computation.10 | async-start | bytes 540672 | tf_op jit(solution)/shard_map/reduce_scatter | solution.py:166
  476.8 51.8 %copy-start.11 = (bf16[2,1024,128]{2,1,0:T(8,128)(2,1)S(1)}, bf16[2,1024,128]{2,1,0:T(8,128)(2,1)}, u32[]{:S(2)}) copy-start(bf16[2,1024,128]{2,1,0:T(8,128)(2,1)} %get-tuple-element.40) | copy-start | bytes 1572868
Sparse Core Ops, SparseCore 0:
  279.8 92.8 reduce-scatter.2
  462.1 62.8 all-gather.2
  528.8 134.4 reduce-scatter.4
where the time goes:
time: 678 us; the launch traced here: 671 us
  waiting for transfers between devices  264 us (39%)
  blocking collectives  146 us (22%)
  local copies, waits for them, and re-layouts  121 us (18%)
  starting transfers between devices  71.9 us (11%)
  matrix products  34.1 us (5%)
  other arithmetic  17.2 us (3%)
  between operations  16.8 us (2%)
    reduce_scatter x1, waiting for transfers between devices, on_device(): lax.psum_scatter(lax.dot_general(columns, grads_flat, (((0,), (0,)), ((),...  119 us
    all_gather x1, blocking collectives, on_device(): lax.all_gather(w_value, 'dp', axis=0, tiled=True)  96.9 us
    all_gather x1, waiting for transfers between devices, on_device(): lax.all_gather(merge_heads(value_back), 'seq', axis=1, tiled=True)  48.1 us
    ppermute x14, starting transfers between devices, swapped(): return lax.ppermute(block, axis, route)  41.2 us
    reduce_scatter x1, waiting for transfers between devices, on_device(): lax.psum_scatter(partial_values.astype(jnp.bfloat16), 'seq', scatter_dime...  38.6 us
    unnamed x31, local copies, waits for them, and re-layouts  38.1 us
    ppermute x14, waiting for transfers between devices, swapped(): return lax.ppermute(block, axis, route)  37.9 us
    all_to_all x1, waiting for transfers between devices, on_device(): lax.all_to_all(blocks, 'seq', split_axis=3, concat_axis=1, tiled=True)  20.3 us
  transfers between devices with their start and end apart: 21, of which 8 were waited for; matrix products, arithmetic and copies ran while one was open for 18% of the time, Pallas kernels for 0%

commit v1 on v0

v1 whole, which is shorter than its diff:
```python
import functools

import jax
import jax.numpy as jnp
from jax import lax
from jax.experimental import pallas as pl
from jax.experimental.pallas import tpu as pltpu
from jax.sharding import PartitionSpec as P

KVH = 4
HD = 128
MESH = pl.DeviceIdType.MESH
ANY = pl.BlockSpec(memory_space=pl.ANY)
VMEM = pl.BlockSpec(memory_space=pltpu.VMEM)
SMEM = pl.BlockSpec(memory_space=pltpu.SMEM)


def remote(src, dst, send_sem, recv_sem, rank, place):
    return pltpu.make_async_remote_copy(
        src_ref=src,
        dst_ref=dst,
        send_sem=send_sem,
        recv_sem=recv_sem,
        device_id=(rank, place),
        device_id_type=MESH,
    )


def each(low, high, body):
    def step(m, carry):
        body(m)
        return carry

    lax.fori_loop(low, high, step, 0)


def greet(n_dp, n_seq, rank, place):
    barrier = pltpu.get_barrier_semaphore()

    def along_seq(m):
        pl.semaphore_signal(
            barrier, inc=1, device_id=(rank, lax.rem(place + m, n_seq)), device_id_type=MESH
        )

    def along_dp(m):
        pl.semaphore_signal(
            barrier, inc=1, device_id=(lax.rem(rank + m, n_dp), place), device_id_type=MESH
        )

    each(1, n_seq, along_seq)
    each(1, n_dp, along_dp)
    pl.semaphore_wait(barrier, n_seq + n_dp - 2)


def aligned(index, size):
    return pl.ds(pl.multiple_of(index * size, size), size)


def gather_kernel(
    n_dp, n_seq, hidden, queries, keys, upstream, w_value, segs,
    q_full, u_full, k_full, v_full, seg_full, x_out,
    perm, y, x, wg, part, other, red, rs, v_own,
    q_send, q_recv, u_send, u_recv, k_send, k_recv, s_send, s_recv, x_send, x_recv,
    w_send, w_recv, e_send, e_recv, r_send, r_recv, v_send, v_recv, local,
):
    rank, place = lax.axis_index("dp"), lax.axis_index("seq")
    rows = queries.shape[1]
    wide = queries.shape[2] // n_seq
    copies = n_seq // KVH
    chips = n_seq // 2
    core, chip = lax.rem(place, 2), place // 2
    quarter, group = lax.rem(place, copies), place // copies
    span = rows * n_seq // copies
    depth = w_value.shape[0]

    greet(n_dp, n_seq, rank, place)

    def seg_copy(m):
        peer = lax.rem(place + m, n_seq)
        return remote(segs, seg_full.at[place], s_send.at[m], s_recv.at[m], rank, peer)

    def w_copy(m):
        peer = lax.rem(rank + m, n_dp)
        return remote(w_value, wg.at[aligned(rank, depth)], w_send.at[m], w_recv.at[m], peer, place)

    def k_copy(m):
        peer = lax.rem(place + m, n_seq)
        return remote(
            keys.at[:, :, aligned(peer // copies, HD)], k_full.at[:, aligned(place, rows), :],
            k_send.at[m], k_recv.at[m], rank, peer,
        )

    def q_copy(m):
        peer = lax.rem(place + m, n_seq)
        return remote(
            queries.at[:, :, aligned(peer, wide)], q_full.at[:, aligned(place, rows), :],
            q_send.at[m], q_recv.at[m], rank, peer,
        )

    def u_copy(m):
        peer = lax.rem(place + m, n_seq)
        return remote(
            upstream.at[:, :, aligned(peer, wide)], u_full.at[:, aligned(place, rows), :],
            u_send.at[m], u_recv.at[m], rank, peer,
        )

    def x_copy(m):
        peer = lax.rem(place + m, n_seq)
        return remote(y.at[peer], x.at[:, aligned(place, rows), :], x_send.at[m], x_recv.at[m], rank, peer)

    each(1, n_seq, lambda m: seg_copy(m).start())
    each(1, n_dp, lambda m: w_copy(m).start())
    each(1, n_seq, lambda m: k_copy(m).start())
    each(1, n_seq, lambda m: q_copy(m).start())
    own = [
        pltpu.make_async_copy(segs, seg_full.at[place], local.at[0]),
        pltpu.make_async_copy(w_value, wg.at[aligned(rank, depth)], local.at[1]),
        pltpu.make_async_copy(
            keys.at[:, :, aligned(group, HD)], k_full.at[:, aligned(place, rows), :], local.at[2]
        ),
        pltpu.make_async_copy(
            queries.at[:, :, aligned(place, wide)], q_full.at[:, aligned(place, rows), :], local.at[3]
        ),
        pltpu.make_async_copy(
            upstream.at[:, :, aligned(place, wide)], u_full.at[:, aligned(place, rows), :], local.at[4]
        ),
    ]
    for copy in own:
        copy.start()

    runs = HD // depth
    size = runs * HD
    i = lax.broadcasted_iota(jnp.int32, (size, size), 0)
    j = lax.broadcasted_iota(jnp.int32, (size, size), 1)
    to = ((i // depth) % runs) * HD + (i // HD) * depth + i % depth
    perm[...] = jnp.where(j == to, 1.0, 0.0).astype(jnp.bfloat16)
    halves = n_seq // runs
    blocks = n_dp // runs
    for half in range(halves):
        for slot in range(2):
            stacked = jnp.concatenate(
                [
                    jnp.concatenate(
                        [
                            hidden[slot, :, ((b * runs + a) * halves + half) * HD : ((b * runs + a) * halves + half + 1) * HD]
                            for a in range(runs)
                        ],
                        1,
                    )
                    for b in range(blocks)
                ],
                0,
            )
            sorted_rows = jnp.dot(stacked, perm[...], preferred_element_type=jnp.float32).astype(jnp.bfloat16)
            for b in range(blocks):
                for a in range(runs):
                    y[half * runs + a, slot, :, b * HD : (b + 1) * HD] = sorted_rows[
                        b * rows : (b + 1) * rows, a * HD : (a + 1) * HD
                    ]
    each(1, n_seq, lambda m: x_copy(m).start())
    own_x = pltpu.make_async_copy(y.at[place], x.at[:, aligned(place, rows), :], local.at[5])
    own_x.start()
    own[1].wait()
    own_x.wait()
    each(1, n_dp, lambda m: w_copy(m).wait_recv())
    each(1, n_seq, lambda m: x_copy(m).wait_recv())
    each(1, n_seq, lambda m: u_copy(m).start())
    keep = pltpu.make_async_copy(x, x_out, local.at[6])
    keep.start()

    def project(n):
        slot, which = n // copies, lax.rem(n, copies)
        part[slot, which // 2, lax.rem(which, 2)] = jnp.dot(
            x[slot, aligned(which, span), :], wg[...], preferred_element_type=jnp.float32
        ).astype(jnp.bfloat16)

    each(0, 2 * copies, project)
    exchange = remote(part.at[:, :, 1 - core], other, e_send.at[0], e_recv.at[0], rank, place + 1 - 2 * core)
    exchange.start()
    exchange.wait_recv()

    def pair_sum(n):
        slot, which = n // 2, lax.rem(n, 2)
        red[slot, which] = (
            part[slot, which, core].astype(jnp.float32) + other[slot, which].astype(jnp.float32)
        ).astype(jnp.bfloat16)

    each(0, copies, pair_sum)

    def r_copy(m):
        peer = lax.rem(chip + m, chips)
        return remote(
            red.at[:, lax.rem(peer, 2), :, aligned(peer // 2, HD)], rs.at[m],
            r_send.at[m], r_recv.at[m], rank, 2 * peer + core,
        )

    each(1, chips, lambda m: r_copy(m).start())
    mine = pltpu.make_async_copy(red.at[:, lax.rem(chip, 2), :, aligned(group, HD)], rs.at[0], local.at[7])
    mine.start()
    mine.wait()
    each(1, chips, lambda m: r_copy(m).wait_recv())
    for slot in range(2):
        total = rs[0, slot].astype(jnp.float32)
        for m in range(1, chips):
            total = total + rs[m, slot].astype(jnp.float32)
        v_own[slot] = total.astype(jnp.bfloat16)

    def v_copy(m):
        peer = group * copies + lax.rem(quarter + m, copies)
        return remote(v_own, v_full.at[:, aligned(quarter, span), :], v_send.at[m], v_recv.at[m], rank, peer)

    each(1, copies, lambda m: v_copy(m).start())
    own_v = pltpu.make_async_copy(v_own, v_full.at[:, aligned(quarter, span), :], local.at[8])
    own_v.start()
    each(1, n_seq, lambda m: seg_copy(m).wait())
    each(1, n_seq, lambda m: k_copy(m).wait())
    each(1, n_seq, lambda m: q_copy(m).wait())
    each(1, n_seq, lambda m: u_copy(m).wait())
    each(1, n_dp, lambda m: w_copy(m).wait_send())
    each(1, n_seq, lambda m: x_copy(m).wait_send())
    exchange.wait_send()
    each(1, chips, lambda m: r_copy(m).wait_send())
    each(1, copies, lambda m: v_copy(m).wait())
    own_v.wait()
    keep.wait()
    for n in (0, 2, 3, 4):
        own[n].wait()


def attention_kernel(q_ref, u_ref, k_ref, v_ref, seg_ref, length_ref, adv_ref, dk_ref, dv_ref, dk_sum, dv_sum):
    slot = pl.program_id(0)
    length = q_ref.shape[1]
    tile = 256
    scale = HD ** (-0.5)
    to_exp2 = scale * 1.4426950408889634
    cut = length - jnp.sum(seg_ref[:, slot, :])
    position = lax.broadcasted_iota(jnp.int32, (length, HD), 0)
    second = position >= cut
    last = jnp.where(second, length - 1, cut - 1)
    sampled = jnp.where(second, length_ref[slot, 1], length_ref[slot, 0])
    gain = jnp.where(second, adv_ref[slot, 1], adv_ref[slot, 0])
    weight = jnp.where(last - position < sampled, gain, jnp.float32(0.0))
    keys, values = k_ref[0], v_ref[0]
    over_last = (((1,), (1,)), ((), ()))
    dk_sum[...] = jnp.zeros_like(dk_sum)
    dv_sum[...] = jnp.zeros_like(dv_sum)
    for head in range(q_ref.shape[2] // HD):
        lanes = slice(head * HD, (head + 1) * HD)
        for block in range(length // tile):
            at = slice(block * tile, (block + 1) * tile)
            seen = (block + 1) * tile
            query = q_ref[0, at, lanes]
            cot = (u_ref[0, at, lanes].astype(jnp.float32) * weight[at]).astype(jnp.bfloat16)
            scores = lax.dot_general(keys[:seen], query, over_last, preferred_element_type=jnp.float32)
            j = lax.broadcasted_iota(jnp.int32, (seen, tile), 0)
            i = lax.broadcasted_iota(jnp.int32, (1, tile), 1) + block * tile
            least = jnp.where(i >= cut, cut, 0)
            scores = jnp.where((j >= least) & (j <= i), scores, jnp.float32(-1e30))
            highest = jnp.max(scores, 0, keepdims=True)
            weighted = jnp.exp2((scores - highest) * to_exp2)
            probs = weighted * (1.0 / jnp.sum(weighted, 0, keepdims=True))
            dprobs = lax.dot_general(values[:seen], cot, over_last, preferred_element_type=jnp.float32)
            dscores = probs * (dprobs - jnp.sum(probs * dprobs, 0, keepdims=True))
            dv_sum[:seen] += jnp.dot(probs.astype(jnp.bfloat16), cot, preferred_element_type=jnp.float32)
            dk_sum[:seen] += jnp.dot(dscores.astype(jnp.bfloat16), query, preferred_element_type=jnp.float32)
    dk_ref[0] = (dk_sum[...] * scale).astype(jnp.bfloat16)
    dv_ref[0] = dv_sum[...].astype(jnp.bfloat16)


def reduce_kernel(
    n_dp, n_seq, plan, dk_part, dv_part, x_ref,
    key_out, weight_out,
    dv_got, vg, dk_got, kg, give, got, dw, dw_got,
    g_send, g_recv, k_send, k_recv, a_send, a_recv, f_send, f_recv, t_send, t_recv, w_send, w_recv, local,
):
    rank, place = lax.axis_index("dp"), lax.axis_index("seq")
    length = dk_part.shape[1]
    rows = length // n_seq
    copies = n_seq // KVH
    chips = n_seq // 2
    core, chip = lax.rem(place, 2), place // 2
    quarter, group = lax.rem(place, copies), place // copies
    span = length // copies
    sibling = place + 1 - 2 * core
    depth = dw.shape[1]

    greet(n_dp, n_seq, rank, place)

    def g_copy(m):
        which = lax.rem(quarter + m, copies)
        return remote(
            dv_part.at[:, aligned(which, span), :], dv_got.at[m],
            g_send.at[m], g_recv.at[m], rank, group * copies + which,
        )

    def k_copy(m):
        peer = lax.rem(place + m, n_seq)
        return remote(
            dk_part.at[:, aligned(peer, rows), :], dk_got.at[place], k_send.at[m], k_recv.at[m], rank, peer
        )

    each(1, copies, lambda m: g_copy(m).start())
    each(1, n_seq, lambda m: k_copy(m).start())
    own_dk = pltpu.make_async_copy(dk_part.at[:, aligned(place, rows), :], dk_got.at[place], local.at[0])
    own_dk.start()
    own_dv = pltpu.make_async_copy(dv_part.at[:, aligned(quarter, span), :], dv_got.at[0], local.at[1])
    own_dv.start()
    own_dv.wait()
    each(1, copies, lambda m: g_copy(m).wait_recv())
    for slot in range(2):
        total = dv_got[0, slot].astype(jnp.float32)
        for m in range(1, copies):
            total = total + dv_got[m, slot].astype(jnp.float32)
        vg[place, slot] = total.astype(jnp.bfloat16)

    def a_copy(m):
        peer = lax.rem(chip + m, chips)
        return remote(vg.at[place], vg.at[place], a_send.at[m], a_recv.at[m], rank, 2 * peer + core)

    def f_copy(m):
        origin = 2 * lax.rem(chip - m + chips, chips) + core
        return remote(vg.at[origin], vg.at[origin], f_send.at[m], f_recv.at[m], rank, sibling)

    each(1, chips, lambda m: a_copy(m).start())
    f_copy(0).start()

    own_dk.wait()
    each(1, n_seq, lambda m: k_copy(m).wait_recv())
    for slot in range(2):
        for head in range(KVH):
            total = dk_got[head * copies, slot].astype(jnp.float32)
            for m in range(1, copies):
                total = total + dk_got[head * copies + m, slot].astype(jnp.float32)
            kg[slot, :, head * HD : (head + 1) * HD] = total.astype(jnp.bfloat16)

    def trade(section):
        low = lax.rem(rank // (1 << section), 2)
        partner = rank + (1 << section) * (1 - 2 * low)
        return remote(
            give.at[section], got.at[section], t_send.at[section], t_recv.at[section], partner, place
        )

    def offer(section):
        giving = jnp.full(kg.shape[1:], plan[rank, section], jnp.int32)
        first, second = kg[0].astype(jnp.float32), kg[1].astype(jnp.float32)
        give[section] = jnp.where(giving == 1, second, first).astype(jnp.bfloat16)
        trade(section).start()

    def accept(section):
        trade(section).wait_recv()
        giving = jnp.full(kg.shape[1:], plan[rank, section], jnp.int32)
        for slot in range(2):
            arrived, held = got[section].astype(jnp.float32), kg[slot].astype(jnp.float32)
            kg[slot] = jnp.where(giving == slot, arrived, held).astype(jnp.bfloat16)

    offer(0)

    def forward(m):
        a_copy(m).wait_recv()
        f_copy(m).start()

    each(1, chips, forward)
    accept(0)
    offer(1)
    each(0, chips, lambda m: f_copy(m).wait_recv())

    total = None
    for slot in range(2):
        for which in range(copies):
            grads = jnp.concatenate([vg[head * copies + which, slot] for head in range(KVH)], 1)
            term = lax.dot_general(
                x_ref[slot, which * span : (which + 1) * span, :], grads,
                (((0,), (0,)), ((), ())), preferred_element_type=jnp.float32,
            )
            total = term if total is None else total + term
    dw[...] = total.astype(jnp.bfloat16).reshape(dw.shape)

    def w_copy(m):
        peer = lax.rem(rank + m, n_dp)
        return remote(dw.at[peer], dw_got.at[m], w_send.at[m], w_recv.at[m], peer, place)

    each(1, n_dp, lambda m: w_copy(m).start())
    accept(1)
    key_out[...] = kg[...]
    total = dw[rank].astype(jnp.float32)
    each(1, n_dp, lambda m: w_copy(m).wait_recv())
    total = lax.fori_loop(1, n_dp, lambda m, t: t + dw_got[m].astype(jnp.float32), total)
    weight_out[...] = total

    each(1, copies, lambda m: g_copy(m).wait_send())
    each(1, n_seq, lambda m: k_copy(m).wait_send())
    each(1, chips, lambda m: a_copy(m).wait_send())
    each(0, chips, lambda m: f_copy(m).wait_send())
    each(1, n_dp, lambda m: w_copy(m).wait_send())
    trade(0).wait_send()
    trade(1).wait_send()


def on_device(
    hidden, queries, keys, upstream, w_value, segment_ids, response_lengths, advantages, move_plan
):
    n_dp, n_seq = lax.axis_size("dp"), lax.axis_size("seq")
    slots, rows, features = hidden.shape
    wide = queries.shape[2] // n_seq
    length = rows * n_seq
    copies = n_seq // KVH
    chips = n_seq // 2
    span = length // copies
    depth, columns = w_value.shape
    width = depth * n_dp
    bf16 = jnp.bfloat16
    dma = pltpu.SemaphoreType.DMA
    square = (HD // depth) * HD

    q_full, u_full, k_full, v_full, seg_full, x_full = pl.pallas_call(
        functools.partial(gather_kernel, n_dp, n_seq),
        out_shape=(
            jax.ShapeDtypeStruct((slots, length, wide), bf16),
            jax.ShapeDtypeStruct((slots, length, wide), bf16),
            jax.ShapeDtypeStruct((slots, length, HD), bf16),
            jax.ShapeDtypeStruct((slots, length, HD), bf16),
            jax.ShapeDtypeStruct((n_seq, slots, rows), jnp.int32),
            jax.ShapeDtypeStruct((slots, length, width), bf16),
        ),
        in_specs=[VMEM, ANY, ANY, ANY, VMEM, VMEM],
        out_specs=[ANY] * 6,
        scratch_shapes=[
            pltpu.VMEM((square, square), bf16),
            pltpu.VMEM((n_seq, slots, rows, width), bf16),
            pltpu.VMEM((slots, length, width), bf16),
            pltpu.VMEM((width, columns), bf16),
            pltpu.VMEM((slots, copies // 2, 2, span, columns), bf16),
            pltpu.VMEM((slots, copies // 2, span, columns), bf16),
            pltpu.VMEM((slots, copies // 2, span, columns), bf16),
            pltpu.VMEM((chips, slots, span, HD), bf16),
            pltpu.VMEM((slots, span, HD), bf16),
        ]
        + [dma((n_seq,))] * 10
        + [dma((n_dp,))] * 2
        + [dma((1,))] * 2
        + [dma((chips,))] * 2
        + [dma((copies,))] * 2
        + [dma((9,))],
        compiler_params=pltpu.CompilerParams(
            collective_id=0, has_side_effects=True, vmem_limit_bytes=40 << 20
        ),
        name="gather",
    )(hidden, queries, keys, upstream, w_value, segment_ids)

    block = lambda w: pl.BlockSpec((1, length, w), lambda slot: (slot, 0, 0))
    dk_part, dv_part = pl.pallas_call(
        attention_kernel,
        grid=(slots,),
        out_shape=(
            jax.ShapeDtypeStruct((slots, length, HD), bf16),
            jax.ShapeDtypeStruct((slots, length, HD), bf16),
        ),
        in_specs=[
            block(wide), block(wide), block(HD), block(HD),
            pl.BlockSpec((n_seq, slots, rows), lambda slot: (0, 0, 0)), SMEM, SMEM,
        ],
        out_specs=[block(HD), block(HD)],
        scratch_shapes=[pltpu.VMEM((length, HD), jnp.float32), pltpu.VMEM((length, HD), jnp.float32)],
        compiler_params=pltpu.CompilerParams(vmem_limit_bytes=40 << 20),
        name="attention",
    )(q_full, u_full, k_full, v_full, seg_full, response_lengths, advantages.astype(jnp.float32))

    return pl.pallas_call(
        functools.partial(reduce_kernel, n_dp, n_seq),
        out_shape=(
            jax.ShapeDtypeStruct((slots, rows, columns), bf16),
            jax.ShapeDtypeStruct((depth, columns), jnp.float32),
        ),
        in_specs=[SMEM, VMEM, VMEM, VMEM],
        out_specs=[VMEM, VMEM],
        scratch_shapes=[
            pltpu.VMEM((copies, slots, span, HD), bf16),
            pltpu.VMEM((n_seq, slots, span, HD), bf16),
            pltpu.VMEM((n_seq, slots, rows, HD), bf16),
            pltpu.VMEM((slots, rows, columns), bf16),
            pltpu.VMEM((2, rows, columns), bf16),
            pltpu.VMEM((2, rows, columns), bf16),
            pltpu.VMEM((n_dp, depth, columns), bf16),
            pltpu.VMEM((n_dp, depth, columns), bf16),
        ]
        + [dma((copies,))] * 2
        + [dma((n_seq,))] * 2
        + [dma((chips,))] * 4
        + [dma((2,))] * 2
        + [dma((n_dp,))] * 2
        + [dma((2,))],
        compiler_params=pltpu.CompilerParams(
            collective_id=1, has_side_effects=True, vmem_limit_bytes=40 << 20
        ),
        name="reduce",
    )(move_plan, dk_part, dv_part, x_full)


def solution(mesh):
    placed = (
        P("dp", "seq", None),
        P("dp", "seq", None),
        P("dp", "seq", None),
        P("dp", "seq", None),
        P(("dp", "seq"), None),
        P("dp", "seq"),
        P("dp", None),
        P("dp", None),
        P(),
    )
    return jax.shard_map(
        on_device,
        mesh=mesh,
        in_specs=placed,
        out_specs=(P("dp", "seq", None), P(("dp", "seq"), None)),
        check_vma=False,
    )
```

time: 678 us -> 188 us (0.28)
  the two profiles are of different devices: /device:TPU:6 before, /device:TPU:1 now
where the time goes in v1:
time: 188 us; the launch traced here: 187 us
  Pallas kernels  179 us (95%)
  local copies, waits for them, and re-layouts  7.71 us (4%)
    pallas_call x1, Pallas kernels, on_device(): pl.pallas_call(functools.partial(gather_kernel, n_dp, n_seq), out_shape=(...  100 us
    pallas_call x1, Pallas kernels, on_device(): pl.pallas_call(functools.partial(reduce_kernel, n_dp, n_seq), out_shape=(...  66.2 us
    pallas_call x1, Pallas kernels, on_device(): pl.pallas_call(attention_kernel, grid=(slots,), out_shape=(jax.ShapeDtype...  12.7 us
    unnamed x21, local copies, waits for them, and re-layouts  7.71 us

profile of v1, /device:TPU:1, one launch (start us, length us, event | category | flops | bytes accessed | tf_op | source)
XLA Modules:
  0.0 187.3 jit_solution(10767823068409236362)
XLA Ops:
  0.6 0.0 copy-start
  0.6 1.6 copy-done
  2.2 0.0 copy-start.1
  2.2 1.2 copy-done.1
  3.5 0.0 copy-start.2
  3.5 1.2 copy-done.2
  4.7 0.0 copy-start.3
  4.7 0.9 copy-done.3
  5.6 0.0 copy-start.4
  5.6 0.7 copy-done.4
  6.3 0.0 copy-start.5
  6.3 0.7 copy-done.5
  7.0 0.0 copy-start.8
  7.0 0.0 copy-start.6
  7.0 100.0 %gather.1 = (bf16[2,1024,256]{2,1,0:T(8,128)(2,1)S(1)}, bf16[2,1024,256]{2,1,0:T(8,128)(2,1)S(1)}, bf16[2,1024,128]{2,1,0:T(8,128)(2,1)S(1)}, bf16[2,1024,128]{2...) custom-call(bf16[2,64,8192]{2,1,0:T(8,128)(2,1)S(1)} %copy-done, ...), custom_call_target="tpu_custom_call" | custom-call | tf_op jit(solution)/shard_map/gather/pallas_call | solution.py:415
  107.0 0.0 copy-start.7
  107.0 0.0 copy-done.8
  107.0 0.0 copy-done.6
  107.0 12.7 %attention.1 = (bf16[2,1024,128]{2,1,0:T(8,128)(2,1)S(1)}, bf16[2,1024,128]{2,1,0:T(8,128)(2,1)S(1)}) custom-call(bf16[2,1024,256]{2,1,0:T(8,128)(2,1)S(1)} %get-tuple-element.10.q_ref, bf16[2,1024,256]{2,1,0:T(8,128)(2,1)S(1)} %get-tuple-element.11.u_ref, bf16[2,1024,128]{2,1,0:T(8,128)(2,1)S(1)} %get-tuple-element.12.k_ref, ...), custom_call_target="tpu_custom_call" | custom-call | tf_op jit(solution)/shard_map/attention/pallas_call | solution.py:451
  119.7 0.0 copy-done.7
  119.7 0.1 copy.11.plan
  119.8 66.2 %reduce.1 = (bf16[2,64,512]{2,1,0:T(8,128)(2,1)S(1)}, f32[16,512]{1,0:T(8,128)S(1)}) custom-call(s32[32,2]{1,0:T(8,128)S(1)} %copy.11.plan, bf16[2,1024,128]{2,1,0:T(8,128)(2,1)S(1)} %get-tuple-element.15.dk_part, bf16[2,1024,128]{2,1,0:T(8,128)(2,1)S(1)} %get-tuple-element.16.dv_part, bf16[2,1024,512]{2,1,0:T(8,128)(2,1)S(1)} %get-tuple-element.17.x_ref), custom_call_target="tpu_custom_call" | custom-call | tf_op jit(solution)/shard_map/reduce/pallas_call | solution.py:468
  186.0 0.7 copy.14
  186.7 0.6 copy.15
  (1 shorter events, 0.0 us)
Async XLA Ops:
  0.6 1.6 copy-start
  2.2 1.2 copy-start.1
  3.5 1.2 copy-start.2
  4.7 0.9 copy-start.3
  5.6 0.7 copy-start.4
  6.3 0.7 copy-start.5
  7.0 100.0 %copy-start.8 = (bf16[2,2]{1,0:T(2,128)(2,1)S(1)}, bf16[2,2]{1,0:T(2,128)(2,1)}, u32[]{:S(2)}) copy-start(bf16[2,2]{1,0:T(2,128)(2,1)} %param.16) | copy-start | bytes 28
  7.0 100.0 %copy-start.6 = (s32[2,2]{1,0:T(2,128)S(1)}, s32[2,2]{1,0:T(2,128)}, u32[]{:S(2)}) copy-start(s32[2,2]{1,0:T(2,128)} %length_ref.1) | copy-start | bytes 52
  107.0 12.7 %copy-start.7 = (s32[32,2]{0,1:T(2,128)S(1)}, s32[32,2]{0,1:T(2,128)}, u32[]{:S(2)}) copy-start(s32[32,2]{0,1:T(2,128)} %param.17) | copy-start | bytes 772

commit v2 on v0

v2 whole, which is shorter than its diff:
```python
import functools

import jax
import jax.numpy as jnp
from jax import lax
from jax.experimental import pallas as pl
from jax.experimental.pallas import tpu as pltpu
from jax.sharding import PartitionSpec as P

KVH = 4
HD = 128
TILE = 256
MESH = pl.DeviceIdType.MESH
ANY = pl.BlockSpec(memory_space=pl.ANY)
VMEM = pl.BlockSpec(memory_space=pltpu.VMEM)
SMEM = pl.BlockSpec(memory_space=pltpu.SMEM)
OVER_LAST = (((1,), (1,)), ((), ()))
OVER_FIRST = (((0,), (0,)), ((), ()))


def remote(src, dst, send_sem, recv_sem, rank, place):
    return pltpu.make_async_remote_copy(
        src_ref=src,
        dst_ref=dst,
        send_sem=send_sem,
        recv_sem=recv_sem,
        device_id=(rank, place),
        device_id_type=MESH,
    )


def each(low, high, body):
    def step(m, carry):
        body(m)
        return carry

    lax.fori_loop(low, high, step, 0)


class Copies:
    def __init__(self):
        self.groups = {}
        self.landed = set()

    def add(self, name, low, high, make):
        self.groups[name] = (low, high, make)

    def start(self, name, low, high, make):
        self.add(name, low, high, make)
        each(low, high, lambda m: make(m).start())

    def arrive(self, name):
        low, high, make = self.groups[name]
        self.landed.add(name)
        each(low, high, lambda m: make(m).wait_recv())

    def finish(self):
        for name in self.groups:
            if name not in self.landed:
                self.arrive(name)
        for low, high, make in self.groups.values():
            each(low, high, lambda m: make(m).wait_send())


def greet(n_dp, n_seq, rank, place):
    barrier = pltpu.get_barrier_semaphore()

    def along_seq(m):
        pl.semaphore_signal(
            barrier, inc=1, device_id=(rank, lax.rem(place + m, n_seq)), device_id_type=MESH
        )

    def along_dp(m):
        pl.semaphore_signal(
            barrier, inc=1, device_id=(lax.rem(rank + m, n_dp), place), device_id_type=MESH
        )

    each(1, n_seq, along_seq)
    each(1, n_dp, along_dp)
    pl.semaphore_wait(barrier, n_seq + n_dp - 2)


def aligned(index, size):
    return pl.ds(pl.multiple_of(index * size, size), size)


def kernel(
    n_dp, n_seq, hidden, queries, keys, upstream, w_value, segs, lengths, gains, plan,
    key_out, weight_out,
    rows_in, perm, y, x, wg, seg, q, u, k, v, probs,
    part, other, red, rs, dv_sum, dv_give, dv_got, vg, dk_sum, dk_give, dk_got, dk_own,
    kg, give, got, dw_far, dw_came, dw_near, dw_own, dw_got,
    s_send, s_recv, k_send, k_recv, q_send, q_recv, u_send, u_recv, x_send, x_recv,
    w_send, w_recv, e_send, e_recv, r_send, r_recv, a_send, a_recv, f_send, f_recv,
    o_send, o_recv, t_send, t_recv, y_send, y_recv, z_send, z_recv,
    c_send, c_recv, local,
):
    rank, place = lax.axis_index("dp"), lax.axis_index("seq")
    rows = queries.shape[1]
    length = rows * n_seq
    half = length // 2
    wide = q.shape[1]
    per_core = wide // HD
    chips = n_seq // 2
    core, chip = lax.rem(place, 2), place // 2
    sibling = place + 1 - 2 * core
    slot, head = chip // KVH, lax.rem(chip, KVH)
    depth = w_value.shape[0]
    n_z = n_dp // 2
    lane, side = lax.rem(rank, n_z), rank // n_z
    f32, bf16 = jnp.float32, jnp.bfloat16
    scale = HD ** (-0.5)

    copies = Copies()
    load = pltpu.make_async_copy(hidden, rows_in, local.at[0])
    load.start()
    greet(n_dp, n_seq, rank, place)

    def s_copy(m):
        peer = lax.rem(place + m, n_seq)
        return remote(segs, seg.at[place], s_send.at[m], s_recv.at[m], rank, peer)

    def k_part(peer):
        return keys.at[peer // (2 * KVH), :, aligned(lax.rem(peer // 2, KVH), HD)]

    def k_copy(m):
        peer = lax.rem(place + m, n_seq)
        return remote(k_part(peer), k.at[aligned(place, rows)], k_send.at[m], k_recv.at[m], rank, peer)

    def head_part(array, peer):
        return array.at[peer // (2 * KVH), :, aligned(lax.rem(peer, 2 * KVH), wide)]

    def q_copy(m):
        peer = lax.rem(place + m, n_seq)
        return remote(head_part(queries, peer), q.at[aligned(place, rows)], q_send.at[m], q_recv.at[m], rank, peer)

    def u_copy(m):
        peer = lax.rem(place + m, n_seq)
        return remote(head_part(upstream, peer), u.at[aligned(place, rows)], u_send.at[m], u_recv.at[m], rank, peer)

    def w_copy(m):
        peer = lax.rem(rank + m, n_dp)
        return remote(w_value, wg.at[aligned(rank, depth)], w_send.at[m], w_recv.at[m], peer, place)

    def x_copy(m):
        peer = lax.rem(place + m, n_seq)
        return remote(y.at[peer], x.at[:, aligned(place, rows), :], x_send.at[m], x_recv.at[m], rank, peer)

    copies.start("s", 1, n_seq, s_copy)
    copies.start("k", 1, n_seq, k_copy)
    copies.start("q", 1, n_seq, q_copy)
    copies.start("u", 1, n_seq, u_copy)
    copies.start("w", 1, n_dp, w_copy)
    own = [
        pltpu.make_async_copy(segs, seg.at[place], local.at[1]),
        pltpu.make_async_copy(k_part(place), k.at[aligned(place, rows)], local.at[2]),
        pltpu.make_async_copy(head_part(queries, place), q.at[aligned(place, rows)], local.at[3]),
        pltpu.make_async_copy(head_part(upstream, place), u.at[aligned(place, rows)], local.at[4]),
        pltpu.make_async_copy(w_value, wg.at[aligned(rank, depth)], local.at[5]),
    ]
    for copy in own:
        copy.start()

    runs = HD // depth
    size = runs * HD
    i = lax.broadcasted_iota(jnp.int32, (size, size), 0)
    j = lax.broadcasted_iota(jnp.int32, (size, size), 1)
    to = ((i // depth) % runs) * HD + (i // HD) * depth + i % depth
    perm[...] = jnp.where(j == to, 1.0, 0.0).astype(bf16)
    halves = n_seq // runs
    blocks = n_dp // runs
    load.wait()
    for part_of in range(halves):
        for n in range(2):
            stacked = jnp.concatenate(
                [
                    jnp.concatenate(
                        [rows_in[n, :, t * HD : (t + 1) * HD] for t in range(b * runs * halves + part_of, (b + 1) * runs * halves, halves)],
                        1,
                    )
                    for b in range(blocks)
                ],
                0,
            )
            regrouped = jnp.dot(stacked, perm[...], preferred_element_type=f32).astype(bf16)
            for b in range(blocks):
                for a in range(runs):
                    y[part_of * runs + a, n, :, b * HD : (b + 1) * HD] = regrouped[
                        b * rows : (b + 1) * rows, a * HD : (a + 1) * HD
                    ]

    for copy in own:
        copy.wait()
    own_x = pltpu.make_async_copy(y.at[place], x.at[:, aligned(place, rows), :], local.at[6])
    own_x.start()
    copies.arrive("s")
    copies.arrive("k")
    copies.arrive("q")
    copies.start("x", 1, n_seq, x_copy)
    cut = length - jnp.where(slot == 0, jnp.sum(seg[:, 0, :]), jnp.sum(seg[:, 1, :]))

    def parts_of(block):
        return block * TILE, (block + 1) * TILE, TILE * block * (block + 1) // 2

    def probs_of(h):
        lanes = aligned(h, HD)
        for block in range(length // TILE):
            at, seen, offset = parts_of(block)
            scores = lax.dot_general(k[:seen], q[at:seen, lanes], OVER_LAST, preferred_element_type=f32)
            j = lax.broadcasted_iota(jnp.int32, (seen, TILE), 0)
            i = lax.broadcasted_iota(jnp.int32, (1, TILE), 1) + at
            least = jnp.where(i >= cut, cut, 0)
            scores = jnp.where((j >= least) & (j <= i), scores, f32(-1e30))
            highest = jnp.max(scores, 0, keepdims=True)
            weighted = jnp.exp2((scores - highest) * (scale * 1.4426950408889634))
            probs[h, offset : offset + seen] = weighted * (1.0 / jnp.sum(weighted, 0, keepdims=True))

    each(0, per_core, probs_of)

    copies.arrive("u")
    position = lax.broadcasted_iota(jnp.int32, (length, HD), 0)
    second = position >= cut
    last = jnp.where(second, length - 1, cut - 1)
    sampled = jnp.where(second, lengths[slot, 1], lengths[slot, 0])
    gain = jnp.where(second, gains[slot, 1], gains[slot, 0])
    weight = jnp.where(last - position < sampled, gain, f32(0.0))
    for h in range(per_core):
        lanes = slice(h * HD, (h + 1) * HD)
        u[:, lanes] = (u[:, lanes].astype(f32) * weight).astype(bf16)
    dv_sum[...] = jnp.zeros_like(dv_sum)

    def value_grads(h):
        lanes = aligned(h, HD)
        for block in range(length // TILE):
            at, seen, offset = parts_of(block)
            dv_sum[:seen] += jnp.dot(
                probs[h, offset : offset + seen].astype(bf16), u[at:seen, lanes], preferred_element_type=f32
            )

    each(0, per_core, value_grads)

    dv_give[...] = dv_sum[aligned(1 - core, half)].astype(bf16)
    dv_swap = remote(dv_give, dv_got, c_send.at[0], c_recv.at[0], rank, sibling)
    copies.start("dv_swap", 0, 1, lambda m: dv_swap)
    copies.arrive("dv_swap")
    vg[place] = (dv_sum[aligned(core, half)] + dv_got[...].astype(f32)).astype(bf16)

    def a_copy(m):
        peer = lax.rem(chip + m, chips)
        return remote(vg.at[place], vg.at[place], a_send.at[m], a_recv.at[m], rank, 2 * peer + core)

    def f_copy(m):
        origin = 2 * lax.rem(chip - m + chips, chips) + core
        return remote(vg.at[origin], vg.at[origin], f_send.at[m], f_recv.at[m], rank, sibling)

    copies.start("a", 1, chips, a_copy)
    f_copy(0).start()
    copies.add("f", 0, chips, f_copy)

    own_x.wait()
    copies.arrive("w")
    copies.arrive("x")

    def project(n, which):
        part[n, which] = jnp.dot(x[n, aligned(which, half), :], wg[...], preferred_element_type=f32).astype(bf16)

    def e_copy(n):
        return remote(part.at[n, 1 - core], other.at[n], e_send.at[n], e_recv.at[n], rank, sibling)

    def project_far(n):
        project(n, 1 - core)
        e_copy(n).start()

    each(0, 2, project_far)
    copies.add("e", 0, 2, e_copy)
    each(0, 2, lambda n: project(n, core))

    def forward(m):
        a_copy(m).wait_recv()
        f_copy(m).start()

    each(1, chips, forward)
    copies.landed.add("a")

    def pair_sum(n):
        e_copy(n).wait_recv()
        red[n] = (part[n, core].astype(f32) + other[n].astype(f32)).astype(bf16)

    each(0, 2, pair_sum)
    copies.landed.add("e")

    def r_copy(m):
        peer = lax.rem(chip + m, chips)
        return remote(
            red.at[peer // KVH, :, aligned(lax.rem(peer, KVH), HD)], rs.at[m],
            r_send.at[m], r_recv.at[m], rank, 2 * peer + core,
        )

    copies.start("r", 1, chips, r_copy)
    own_r = pltpu.make_async_copy(red.at[slot, :, aligned(head, HD)], rs.at[0], local.at[7])
    own_r.start()

    copies.arrive("f")

    def weight_terms(column, count):
        total = None
        for n in range(2):
            for which in range(2):
                grads = jnp.concatenate([vg[(n * KVH + g) * 2 + which] for g in range(KVH)], 1)
                term = lax.dot_general(
                    x[n, which * half : (which + 1) * half, pl.ds(pl.multiple_of(column, HD), count)], grads,
                    OVER_FIRST, preferred_element_type=f32,
                )
                total = term if total is None else total + term
        return total

    share = n_z * depth
    pieces = share // HD

    def y_copy(n):
        return remote(
            dw_far.at[n], dw_came.at[n], y_send.at[n], y_recv.at[n], lane + n_z * (1 - side), place
        )

    def far_terms(n):
        dw_far[n] = weight_terms((1 - side) * share + n * HD, HD).astype(bf16)
        y_copy(n).start()

    def near_terms(n):
        dw_near[n] = weight_terms(side * share + n * HD, HD)

    each(0, pieces, far_terms)
    copies.add("y", 0, pieces, y_copy)
    each(0, pieces, near_terms)

    def z_copy(m):
        to_lane = lax.rem(lane + m, n_z)
        return remote(dw_own.at[to_lane], dw_got.at[m], z_send.at[m], z_recv.at[m], to_lane + n_z * side, place)

    def merge(n):
        y_copy(n).wait_recv()
        summed = (dw_near[n] + dw_came[n].astype(f32)).astype(bf16)
        dw_own[pl.ds(n * runs, runs)] = summed.reshape(runs, depth, summed.shape[1])

    each(0, pieces, merge)
    copies.landed.add("y")
    copies.start("z", 1, n_z, z_copy)

    own_r.wait()
    copies.arrive("r")
    total = rs[0].astype(f32)
    for m in range(1, chips):
        total = total + rs[m].astype(f32)
    v[aligned(core, half)] = total.astype(bf16)
    v_swap = remote(
        v.at[aligned(core, half)], v.at[aligned(core, half)], c_send.at[1], c_recv.at[1], rank, sibling
    )
    copies.start("v_swap", 0, 1, lambda m: v_swap)
    dk_sum[...] = jnp.zeros_like(dk_sum)
    copies.arrive("v_swap")

    def key_grads(h):
        lanes = aligned(h, HD)
        for block in range(length // TILE):
            at, seen, offset = parts_of(block)
            p = probs[h, offset : offset + seen]
            dprobs = lax.dot_general(v[:seen], u[at:seen, lanes], OVER_LAST, preferred_element_type=f32)
            dscores = p * (dprobs - jnp.sum(p * dprobs, 0, keepdims=True))
            dk_sum[:seen] += jnp.dot(dscores.astype(bf16), q[at:seen, lanes], preferred_element_type=f32)

    each(0, per_core, key_grads)
    dk_give[...] = (dk_sum[aligned(1 - core, half)] * scale).astype(bf16)
    dk_swap = remote(dk_give, dk_got, c_send.at[2], c_recv.at[2], rank, sibling)
    copies.start("dk_swap", 0, 1, lambda m: dk_swap)
    copies.arrive("dk_swap")
    dk_own[...] = (dk_sum[aligned(core, half)] * scale + dk_got[...].astype(f32)).astype(bf16).reshape(dk_own.shape)

    def o_copy(t):
        return remote(
            dk_own.at[t], kg.at[slot, :, aligned(head, HD)], o_send.at[t], o_recv.at[chip],
            rank, core * chips + t,
        )

    def o_start(t):
        @pl.when(core * chips + t != place)
        def _():
            o_copy(t).start()

        @pl.when(core * chips + t == place)
        def _():
            copy = pltpu.make_async_copy(dk_own.at[t], kg.at[slot, :, aligned(head, HD)], local.at[8])
            copy.start()
            copy.wait()

    each(0, chips, o_start)

    def o_wait_recv(c):
        @pl.when(2 * c + place // chips != place)
        def _():
            remote(
                dk_own.at[0], kg.at[c // KVH, :, aligned(lax.rem(c, KVH), HD)], o_send.at[0], o_recv.at[c],
                rank, 2 * c + place // chips,
            ).wait_recv()

    each(0, chips, o_wait_recv)

    def trade(section):
        low = lax.rem(rank // (1 << section), 2)
        partner = rank + (1 << section) * (1 - 2 * low)
        return remote(
            give.at[section], got.at[section], t_send.at[section], t_recv.at[section], partner, place
        )

    for section in range(2):
        giving = jnp.full(kg.shape[1:], plan[section, rank], jnp.int32)
        first, other_slot = kg[0].astype(f32), kg[1].astype(f32)
        give[section] = jnp.where(giving == 1, other_slot, first).astype(bf16)
        copies.start(("t", section), section, section + 1, trade)
        copies.arrive(("t", section))
        arrived = got[section].astype(f32)
        kg[0] = jnp.where(giving == 0, arrived, first).astype(bf16)
        kg[1] = jnp.where(giving == 1, arrived, other_slot).astype(bf16)
    key_out[...] = kg[...]

    copies.arrive("z")
    total = dw_own[lane].astype(f32)
    for m in range(1, n_z):
        total = total + dw_got[m].astype(f32)
    weight_out[...] = total

    def o_wait_send(t):
        @pl.when(core * chips + t != place)
        def _():
            o_copy(t).wait_send()

    each(0, chips, o_wait_send)
    copies.finish()


def on_device(
    hidden, queries, keys, upstream, w_value, segment_ids, response_lengths, advantages, move_plan
):
    n_dp, n_seq = lax.axis_size("dp"), lax.axis_size("seq")
    slots, rows, features = hidden.shape
    length = rows * n_seq
    half = length // 2
    chips = n_seq // 2
    wide = queries.shape[2] * slots // n_seq
    heads = wide // HD
    depth, columns = w_value.shape
    width = depth * n_dp
    share = width // 2
    bf16, f32 = jnp.bfloat16, jnp.float32
    square = (HD // depth) * HD
    tiles = length // TILE
    triangle = TILE * tiles * (tiles + 1) // 2
    dma = pltpu.SemaphoreType.DMA
    return pl.pallas_call(
        functools.partial(kernel, n_dp, n_seq),
        out_shape=(
            jax.ShapeDtypeStruct((slots, rows, columns), bf16),
            jax.ShapeDtypeStruct((depth, columns), f32),
        ),
        in_specs=[ANY, ANY, ANY, ANY, VMEM, VMEM, SMEM, SMEM, SMEM],
        out_specs=[VMEM, VMEM],
        scratch_shapes=[
            pltpu.VMEM((slots, rows, features), bf16),
            pltpu.VMEM((square, square), bf16),
            pltpu.VMEM((n_seq, slots, rows, width), bf16),
            pltpu.VMEM((slots, length, width), bf16),
            pltpu.VMEM((width, columns), bf16),
            pltpu.VMEM((n_seq, slots, rows), jnp.int32),
            pltpu.VMEM((length, wide), bf16),
            pltpu.VMEM((length, wide), bf16),
            pltpu.VMEM((length, HD), bf16),
            pltpu.VMEM((length, HD), bf16),
            pltpu.VMEM((heads, triangle, TILE), f32),
            pltpu.VMEM((slots, 2, half, columns), bf16),
            pltpu.VMEM((slots, half, columns), bf16),
            pltpu.VMEM((slots, half, columns), bf16),
            pltpu.VMEM((chips, half, HD), bf16),
            pltpu.VMEM((length, HD), f32),
            pltpu.VMEM((half, HD), bf16),
            pltpu.VMEM((half, HD), bf16),
            pltpu.VMEM((n_seq, half, HD), bf16),
            pltpu.VMEM((length, HD), f32),
            pltpu.VMEM((half, HD), bf16),
            pltpu.VMEM((half, HD), bf16),
            pltpu.VMEM((chips, rows, HD), bf16),
            pltpu.VMEM((slots, rows, columns), bf16),
            pltpu.VMEM((2, rows, columns), bf16),
            pltpu.VMEM((2, rows, columns), bf16),
            pltpu.VMEM((share // HD, HD, columns), bf16),
            pltpu.VMEM((share // HD, HD, columns), bf16),
            pltpu.VMEM((share // HD, HD, columns), f32),
            pltpu.VMEM((n_dp // 2, depth, columns), bf16),
            pltpu.VMEM((n_dp // 2, depth, columns), bf16),
        ]
        + [dma((n_seq,))] * 10
        + [dma((n_dp,))] * 2
        + [dma((2,))] * 2
        + [dma((chips,))] * 8
        + [dma((2,))] * 4
        + [dma((n_dp // 2,))] * 2
        + [dma((3,))] * 2
        + [dma((9,))],
        compiler_params=pltpu.CompilerParams(
            collective_id=0, has_side_effects=True, vmem_limit_bytes=60 << 20
        ),
        name="backward",
    )(
        hidden, queries, keys, upstream, w_value, segment_ids, response_lengths,
        advantages.astype(f32), move_plan.T,
    )


def solution(mesh):
    placed = (
        P("dp", "seq", None),
        P("dp", "seq", None),
        P("dp", "seq", None),
        P("dp", "seq", None),
        P(("dp", "seq"), None),
        P("dp", "seq"),
        P("dp", None),
        P("dp", None),
        P(),
    )
    return jax.shard_map(
        on_device,
        mesh=mesh,
        in_specs=placed,
        out_specs=(P("dp", "seq", None), P(("dp", "seq"), None)),
        check_vma=False,
    )
```

time: 678 us -> 142 us (0.21)
  the two profiles are of different devices: /device:TPU:6 before, /device:TPU:1 now
where the time goes in v2:
time: 142 us; the launch traced here: 140 us
  Pallas kernels  136 us (96%)
  local copies, waits for them, and re-layouts  2.94 us (2%)
    pallas_call x1, Pallas kernels, on_device(): pl.pallas_call(functools.partial(kernel, n_dp, n_seq), out_shape=(jax.Sha...  136 us
    unnamed x2, local copies, waits for them, and re-layouts  2.94 us

profile of v2, /device:TPU:1, one launch (start us, length us, event | category | flops | bytes accessed | tf_op | source)
XLA Modules:
  0.0 140.5 jit_solution(2319944393573321553)
XLA Ops:
  0.6 1.2 convert_element_type.3.gains
  1.8 135.7 %backward.1 = (bf16[2,64,512]{2,1,0:T(8,128)(2,1)}, f32[16,512]{1,0:T(8,128)}) custom-call(bf16[2,64,8192]{2,1,0:T(8,128)(2,1)} %hidden.1, bf16[2,64,4096]{2,1,0:T(8,128)(2,1)} %queries.1, bf16[2,64,512]{2,1,0:T(8,128)(2,1)} %keys.1, bf16[2,64,4096]{2,1,0:T(8,128)(2,1)} %upstream.1, bf16[16,512]{1,0:T(8,128)(2,1)} %w_value.1, s32[2,64]{1,0:T(2,128)} %segs.1, ...), custom_call_target="tpu_custom_call" | custom-call | tf_op jit(solution)/shard_map/backward/pallas_call | solution.py:458
  137.5 1.6 %copy.13 = bf16[2,64,512]{2,1,0:T(8,128)(2,1)} copy(bf16[2,64,512]{2,1,0:T(8,128)(2,1)} %get-tuple-element.4) | data formatting | bytes 262144
  139.1 1.4 copy.14

commit v3 on v2

v3 whole, which is shorter than its diff:
```python
import functools

import jax
import jax.numpy as jnp
from jax import lax
from jax.experimental import pallas as pl
from jax.experimental.pallas import tpu as pltpu
from jax.sharding import PartitionSpec as P

KVH = 4
HD = 128
TILE = 256
MESH = pl.DeviceIdType.MESH
ANY = pl.BlockSpec(memory_space=pl.ANY)
VMEM = pl.BlockSpec(memory_space=pltpu.VMEM)
SMEM = pl.BlockSpec(memory_space=pltpu.SMEM)
OVER_LAST = (((1,), (1,)), ((), ()))
OVER_FIRST = (((0,), (0,)), ((), ()))


def remote(src, dst, send_sem, recv_sem, rank, place):
    return pltpu.make_async_remote_copy(
        src_ref=src,
        dst_ref=dst,
        send_sem=send_sem,
        recv_sem=recv_sem,
        device_id=(rank, place),
        device_id_type=MESH,
    )


def each(low, high, body):
    def step(m, carry):
        body(m)
        return carry

    lax.fori_loop(low, high, step, 0)


class Copies:
    def __init__(self):
        self.groups = {}
        self.landed = set()

    def add(self, name, low, high, make):
        self.groups[name] = (low, high, make)

    def start(self, name, low, high, make):
        self.add(name, low, high, make)
        each(low, high, lambda m: make(m).start())

    def arrive(self, name):
        low, high, make = self.groups[name]
        self.landed.add(name)
        each(low, high, lambda m: make(m).wait_recv())

    def settle(self, *names):
        for name in names:
            low, high, make = self.groups.pop(name)
            each(low, high, lambda m: make(m).wait_send())

    def finish(self):
        self.settle(*self.groups)


def greet(n_dp, n_seq, rank, place):
    barrier = pltpu.get_barrier_semaphore()

    def along_seq(m):
        pl.semaphore_signal(
            barrier, inc=1, device_id=(rank, lax.rem(place + m, n_seq)), device_id_type=MESH
        )

    def along_dp(m):
        pl.semaphore_signal(
            barrier, inc=1, device_id=(lax.rem(rank + m, n_dp), place), device_id_type=MESH
        )

    each(1, n_seq, along_seq)
    each(1, n_dp, along_dp)
    pl.semaphore_wait(barrier, n_seq + n_dp - 2)


def aligned(index, size):
    return pl.ds(pl.multiple_of(index * size, size), size)


def kernel(
    n_dp, n_seq, hidden, queries, keys, upstream, w_value, segs, lengths, gains, plan,
    key_out, weight_out,
    rows_in, perm, y, x, wg, seg, q, u, k, v, probs,
    part, other, red, rs, dv_sum, dv_give, dv_got, vg, dk_sum, dk_own,
    kgs, kg, give, got, dw_far, dw_came, dw_near, dw_own, dw_got,
    s_send, s_recv, k_send, k_recv, q_send, q_recv, u_send, u_recv, o_send, o_recv, x_send, x_recv,
    w_send, w_recv, e_send, e_recv, p_send, p_recv, r_send, r_recv, a_send, a_recv, f_send, f_recv,
    t_send, t_recv, y_send, y_recv, z_send, z_recv,
    c_send, c_recv, local,
):
    rank, place = lax.axis_index("dp"), lax.axis_index("seq")
    rows = queries.shape[1]
    length = rows * n_seq
    half = length // 2
    wide = q.shape[1]
    per_core = wide // HD
    chips = n_seq // 2
    core, chip = lax.rem(place, 2), place // 2
    sibling = place + 1 - 2 * core
    slot, head = chip // KVH, lax.rem(chip, KVH)
    depth = w_value.shape[0]
    n_z = n_dp // 2
    lane, side = lax.rem(rank, n_z), rank // n_z
    f32, bf16 = jnp.float32, jnp.bfloat16
    scale = HD ** (-0.5)

    copies = Copies()
    load = pltpu.make_async_copy(hidden, rows_in, local.at[0])
    load.start()
    greet(n_dp, n_seq, rank, place)

    def s_copy(m):
        peer = lax.rem(place + m, n_seq)
        return remote(segs, seg.at[place], s_send.at[m], s_recv.at[m], rank, peer)

    def k_part(peer):
        return keys.at[peer // (2 * KVH), :, aligned(lax.rem(peer // 2, KVH), HD)]

    def k_copy(m):
        peer = 2 * lax.rem(chip + m, chips) + core
        return remote(k_part(peer), k.at[aligned(place, rows)], k_send.at[m], k_recv.at[m], rank, peer)

    def k_pass(n):
        origin = 2 * n + core
        return remote(
            k.at[aligned(origin, rows)], k.at[aligned(origin, rows)], p_send.at[n], p_recv.at[n], rank, sibling
        )

    def head_part(array, peer):
        return array.at[peer // (2 * KVH), :, aligned(lax.rem(peer, 2 * KVH), wide)]

    def q_copy(m):
        peer = lax.rem(place + m, n_seq)
        return remote(head_part(queries, peer), q.at[aligned(place, rows)], q_send.at[m], q_recv.at[m], rank, peer)

    def u_copy(m):
        peer = lax.rem(place + m, n_seq)
        return remote(head_part(upstream, peer), u.at[aligned(place, rows)], u_send.at[m], u_recv.at[m], rank, peer)

    def w_copy(m):
        peer = lax.rem(rank + m, n_dp)
        return remote(w_value, wg.at[aligned(rank, depth)], w_send.at[m], w_recv.at[m], peer, place)

    def x_copy(m):
        peer = lax.rem(place + m, n_seq)
        n = m // n_seq
        peer = lax.rem(place + m, n_seq)
        return remote(y.at[n, peer], x.at[n, aligned(place, rows), :], x_send.at[m], x_recv.at[m], rank, peer)

    own = [
        pltpu.make_async_copy(segs, seg.at[place], local.at[1]),
        pltpu.make_async_copy(k_part(place), k.at[aligned(place, rows)], local.at[2]),
        pltpu.make_async_copy(head_part(queries, place), q.at[aligned(place, rows)], local.at[3]),
        pltpu.make_async_copy(head_part(upstream, place), u.at[aligned(place, rows)], local.at[4]),
        pltpu.make_async_copy(w_value, wg.at[aligned(rank, depth)], local.at[5]),
    ]

    def send_keys():
        copies.start("s", 1, n_seq, s_copy)
        copies.start("k", 1, chips, k_copy)

    def send_queries():
        copies.start("q", 1, n_seq, q_copy)

    def send_upstream():
        copies.start("u", 1, n_seq, u_copy)

    def send_weights():
        copies.start("w", 1, n_dp, w_copy)
        for copy in own:
            copy.start()

    own_x = [
        pltpu.make_async_copy(y.at[n, place], x.at[n, aligned(place, rows), :], local.at[6 + n]) for n in range(2)
    ]
    runs = HD // depth

    def regroup():
        size = runs * HD
        i = lax.broadcasted_iota(jnp.int32, (size, size), 0)
        j = lax.broadcasted_iota(jnp.int32, (size, size), 1)
        to = ((i // depth) % runs) * HD + (i // HD) * depth + i % depth
        perm[...] = jnp.where(j == to, 1.0, 0.0).astype(bf16)
        halves = n_seq // runs
        blocks = n_dp // runs
        load.wait()
        for part_of in range(halves):
            for n in range(2):
                stacked = jnp.concatenate(
                    [
                        jnp.concatenate(
                            [
                                rows_in[n, :, t * HD : (t + 1) * HD]
                                for t in range(b * runs * halves + part_of, (b + 1) * runs * halves, halves)
                            ],
                            1,
                        )
                        for b in range(blocks)
                    ],
                    0,
                )
                regrouped = jnp.dot(stacked, perm[...], preferred_element_type=f32).astype(bf16)
                for b in range(blocks):
                    for a in range(runs):
                        y[n, part_of * runs + a, :, b * HD : (b + 1) * HD] = regrouped[
                            b * rows : (b + 1) * rows, a * HD : (a + 1) * HD
                        ]
        for copy in own:
            copy.wait()

    def send_hidden(n):
        copies.start(("x", n), n * n_seq + 1, (n + 1) * n_seq, x_copy)
        own_x[n].start()

    def parts_of(block):
        return block * TILE, (block + 1) * TILE, TILE * block * (block + 1) // 2

    def find_cut():
        return length - jnp.where(slot == 0, jnp.sum(seg[:, 0, :]), jnp.sum(seg[:, 1, :]))

    def make_probs():
        for name in "skq":
            copies.arrive(name)
            if name == "k":
                copies.start("p", 0, chips, k_pass)
        send_hidden(1)
        copies.arrive("p")
        cut = find_cut()

        def of_head(h):
            lanes = aligned(h, HD)
            for block in range(length // TILE):
                at, seen, offset = parts_of(block)
                scores = lax.dot_general(k[:seen], q[at:seen, lanes], OVER_LAST, preferred_element_type=f32)
                j = lax.broadcasted_iota(jnp.int32, (seen, TILE), 0)
                i = lax.broadcasted_iota(jnp.int32, (1, TILE), 1) + at
                least = jnp.where(i >= cut, cut, 0)
                scores = jnp.where((j >= least) & (j <= i), scores, f32(-1e30))
                highest = jnp.max(scores, 0, keepdims=True)
                weighted = jnp.exp2((scores - highest) * (scale * 1.4426950408889634))
                probs[h, offset : offset + seen] = weighted * (1.0 / jnp.sum(weighted, 0, keepdims=True))

        each(0, per_core, of_head)

    dv_swap = remote(dv_give, dv_got, c_send.at[0], c_recv.at[0], rank, sibling)

    def make_value_grads():
        copies.arrive("u")
        cut = find_cut()
        position = lax.broadcasted_iota(jnp.int32, (length, HD), 0)
        second = position >= cut
        last = jnp.where(second, length - 1, cut - 1)
        sampled = jnp.where(second, lengths[slot, 1], lengths[slot, 0])
        table = gains[...].astype(f32)
        table = jnp.where(slot == 0, table[0:1], table[1:2])
        gain = jnp.where(second, table[0:1, 1:2], table[0:1, 0:1])
        weight = jnp.where(last - position < sampled, gain, f32(0.0))
        for h in range(per_core):
            lanes = slice(h * HD, (h + 1) * HD)
            u[:, lanes] = (u[:, lanes].astype(f32) * weight).astype(bf16)
        dv_sum[...] = jnp.zeros_like(dv_sum)

        def of_head(h):
            lanes = aligned(h, HD)
            for block in range(length // TILE):
                at, seen, offset = parts_of(block)
                dv_sum[:seen] += jnp.dot(
                    probs[h, offset : offset + seen].astype(bf16), u[at:seen, lanes], preferred_element_type=f32
                )

        each(0, per_core, of_head)
        dv_give[...] = dv_sum[aligned(1 - core, half)].astype(bf16)
        copies.start("dv_swap", 0, 1, lambda m: dv_swap)

    def a_copy(m):
        peer = lax.rem(chip + m, chips)
        return remote(vg.at[place], vg.at[place], a_send.at[m], a_recv.at[m], rank, 2 * peer + core)

    def f_copy(m):
        origin = 2 * lax.rem(chip - m + chips, chips) + core
        return remote(vg.at[origin], vg.at[origin], f_send.at[m], f_recv.at[m], rank, sibling)

    def send_value_grads():
        copies.arrive("dv_swap")
        vg[place] = (dv_sum[aligned(core, half)] + dv_got[...].astype(f32)).astype(bf16)
        copies.start("a", 1, chips, a_copy)
        f_copy(0).start()
        copies.add("f", 0, chips, f_copy)

    def forward_value_grads():
        def forward(m):
            a_copy(m).wait_recv()
            f_copy(m).start()

        each(1, chips, forward)
        copies.landed.add("a")

    def project(n, which):
        part[n, which] = jnp.dot(x[n, aligned(which, half), :], wg[...], preferred_element_type=f32).astype(bf16)

    def e_copy(n):
        return remote(part.at[n, 1 - core], other.at[n], e_send.at[n], e_recv.at[n], rank, sibling)

    def project_values(n):
        if n == 0:
            copies.arrive("w")
        own_x[n].wait()
        copies.arrive(("x", n))
        project(n, 1 - core)
        copies.start(("e", n), n, n + 1, e_copy)
        project(n, core)

    def r_copy(m):
        peer = lax.rem(chip + m, chips)
        return remote(
            red.at[peer // KVH, :, aligned(lax.rem(peer, KVH), HD)], rs.at[m],
            r_send.at[m], r_recv.at[m], rank, 2 * peer + core,
        )

    own_r = pltpu.make_async_copy(red.at[slot, :, aligned(head, HD)], rs.at[0], local.at[8])

    def send_partials():
        for n in range(2):
            copies.arrive(("e", n))
            red[n] = (part[n, core].astype(f32) + other[n].astype(f32)).astype(bf16)
        copies.start("r", 1, chips, r_copy)
        own_r.start()

    v_swap = remote(
        v.at[aligned(core, half)], v.at[aligned(core, half)], c_send.at[1], c_recv.at[1], rank, sibling
    )

    def sum_values():
        own_r.wait()
        copies.arrive("r")
        total = rs[0].astype(f32)
        for m in range(1, chips):
            total = total + rs[m].astype(f32)
        v[aligned(core, half)] = total.astype(bf16)
        copies.start("v_swap", 0, 1, lambda m: v_swap)

    def o_copy(m):
        peer = lax.rem(place + m, n_seq)
        return remote(
            dk_own.at[aligned(peer, rows)], kgs.at[core, slot, :, aligned(head, HD)],
            o_send.at[m], o_recv.at[m], rank, peer,
        )

    own_o = pltpu.make_async_copy(
        dk_own.at[aligned(place, rows)], kgs.at[core, slot, :, aligned(head, HD)], local.at[9]
    )

    def make_key_grads():
        dk_sum[...] = jnp.zeros_like(dk_sum)
        copies.arrive("v_swap")

        def of_head(h):
            lanes = aligned(h, HD)
            for block in range(length // TILE):
                at, seen, offset = parts_of(block)
                p = probs[h, offset : offset + seen]
                dprobs = lax.dot_general(v[:seen], u[at:seen, lanes], OVER_LAST, preferred_element_type=f32)
                dscores = p * (dprobs - jnp.sum(p * dprobs, 0, keepdims=True))
                dk_sum[:seen] += jnp.dot(dscores.astype(bf16), q[at:seen, lanes], preferred_element_type=f32)

        each(0, per_core, of_head)
        dk_own[...] = (dk_sum[...] * scale).astype(bf16)
        copies.start("o", 1, n_seq, o_copy)
        own_o.start()

    def trade(section):
        low = lax.rem(rank // (1 << section), 2)
        partner = rank + (1 << section) * (1 - 2 * low)
        return remote(
            give.at[section], got.at[section], t_send.at[section], t_recv.at[section], partner, place
        )

    def chosen(section):
        return jnp.full(kg.shape[1:], plan[section, rank], jnp.int32)

    def offer(section):
        first, second = kg[0].astype(f32), kg[1].astype(f32)
        give[section] = jnp.where(chosen(section) == 1, second, first).astype(bf16)
        copies.start(("t", section), section, section + 1, trade)

    def accept(section):
        copies.arrive(("t", section))
        giving = chosen(section)
        arrived = got[section].astype(f32)
        for n in range(2):
            kg[n] = jnp.where(giving == n, arrived, kg[n].astype(f32)).astype(bf16)

    def first_trade():
        own_o.wait()
        copies.arrive("o")
        kg[...] = (kgs[0].astype(f32) + kgs[1].astype(f32)).astype(bf16)
        offer(0)

    def second_trade():
        accept(0)
        offer(1)

    def end_trade():
        accept(1)
        key_out[...] = kg[...]

    def weight_terms(column, count):
        total = None
        for n in range(2):
            for which in range(2):
                grads = jnp.concatenate([vg[(n * KVH + g) * 2 + which] for g in range(KVH)], 1)
                term = lax.dot_general(
                    x[n, which * half : (which + 1) * half, pl.ds(pl.multiple_of(column, HD), count)], grads,
                    OVER_FIRST, preferred_element_type=f32,
                )
                total = term if total is None else total + term
        return total

    share = n_z * depth
    pieces, piece = dw_far.shape[0], dw_far.shape[2]

    def y_copy(n):
        return remote(
            dw_far.at[n], dw_came.at[n], y_send.at[n], y_recv.at[n], lane + n_z * (1 - side), place
        )

    def make_weight_grads():
        copies.arrive("f")

        def far(n):
            terms = weight_terms((1 - side) * share + n * HD, HD).astype(bf16)
            for c in range(pieces):
                dw_far[c, aligned(n, HD)] = terms[:, c * piece : (c + 1) * piece]

        def near(n):
            dw_near[aligned(n, HD)] = weight_terms(side * share + n * HD, HD)

        each(0, share // HD, far)
        copies.start("y", 0, pieces, y_copy)
        each(0, share // HD, near)

    def z_copy(m):
        to_lane = lax.rem(lane + m, n_z)
        return remote(
            dw_own.at[m // n_z, to_lane], dw_got.at[m], z_send.at[m], z_recv.at[m], to_lane + n_z * side, place
        )

    def send_weight_grads():
        for c in range(pieces):
            y_copy(c).wait_recv()
            summed = (dw_near[:, c * piece : (c + 1) * piece] + dw_came[c].astype(f32)).astype(bf16)
            dw_own[c] = summed.reshape(n_z, depth, piece)
            copies.start(("z", c), c * n_z + 1, (c + 1) * n_z, z_copy)
        copies.landed.add("y")

    def sum_weight_grads():
        for c in range(pieces):
            copies.arrive(("z", c))
            total = dw_own[c, lane].astype(f32)
            for m in range(c * n_z + 1, (c + 1) * n_z):
                total = total + dw_got[m].astype(f32)
            weight_out[:, c * piece : (c + 1) * piece] = total

    send_keys()
    send_queries()
    send_upstream()
    send_weights()
    regroup()
    send_hidden(0)
    make_probs()
    make_value_grads()
    project_values(0)
    send_value_grads()
    project_values(1)
    forward_value_grads()
    send_partials()
    copies.settle("s", "k", "p", "q", "u", "w", ("x", 0), ("x", 1), ("e", 0), ("e", 1))
    make_weight_grads()
    sum_values()
    send_weight_grads()
    make_key_grads()
    first_trade()
    copies.settle("a", "f", "r", "y", "dv_swap", "v_swap", "o")
    second_trade()
    end_trade()
    sum_weight_grads()
    copies.finish()


def on_device(
    hidden, queries, keys, upstream, w_value, segment_ids, response_lengths, advantages, move_plan
):
    n_dp, n_seq = lax.axis_size("dp"), lax.axis_size("seq")
    slots, rows, features = hidden.shape
    length = rows * n_seq
    half = length // 2
    chips = n_seq // 2
    wide = queries.shape[2] * slots // n_seq
    heads = wide // HD
    depth, columns = w_value.shape
    width = depth * n_dp
    share = width // 2
    bf16, f32 = jnp.bfloat16, jnp.float32
    square = (HD // depth) * HD
    tiles = length // TILE
    triangle = TILE * tiles * (tiles + 1) // 2
    dma = pltpu.SemaphoreType.DMA
    return pl.pallas_call(
        functools.partial(kernel, n_dp, n_seq),
        out_shape=(
            jax.ShapeDtypeStruct((slots, rows, columns), bf16),
            jax.ShapeDtypeStruct((depth, columns), f32),
        ),
        in_specs=[ANY, ANY, ANY, ANY, VMEM, VMEM, SMEM, VMEM, SMEM],
        out_specs=[VMEM, VMEM],
        scratch_shapes=[
            pltpu.VMEM((slots, rows, features), bf16),
            pltpu.VMEM((square, square), bf16),
            pltpu.VMEM((slots, n_seq, rows, width), bf16),
            pltpu.VMEM((slots, length, width), bf16),
            pltpu.VMEM((width, columns), bf16),
            pltpu.VMEM((n_seq, slots, rows), jnp.int32),
            pltpu.VMEM((length, wide), bf16),
            pltpu.VMEM((length, wide), bf16),
            pltpu.VMEM((length, HD), bf16),
            pltpu.VMEM((length, HD), bf16),
            pltpu.VMEM((heads, triangle, TILE), f32),
            pltpu.VMEM((slots, 2, half, columns), bf16),
            pltpu.VMEM((slots, half, columns), bf16),
            pltpu.VMEM((slots, half, columns), bf16),
            pltpu.VMEM((chips, half, HD), bf16),
            pltpu.VMEM((length, HD), f32),
            pltpu.VMEM((half, HD), bf16),
            pltpu.VMEM((half, HD), bf16),
            pltpu.VMEM((n_seq, half, HD), bf16),
            pltpu.VMEM((length, HD), f32),
            pltpu.VMEM((length, HD), bf16),
            pltpu.VMEM((2, slots, rows, columns), bf16),
            pltpu.VMEM((slots, rows, columns), bf16),
            pltpu.VMEM((2, rows, columns), bf16),
            pltpu.VMEM((2, rows, columns), bf16),
            pltpu.VMEM((2, share, columns // 2), bf16),
            pltpu.VMEM((2, share, columns // 2), bf16),
            pltpu.VMEM((share, columns), f32),
            pltpu.VMEM((2, n_dp // 2, depth, columns // 2), bf16),
            pltpu.VMEM((n_dp, depth, columns // 2), bf16),
        ]
        + [dma((n_seq,))] * 10 + [dma((2 * n_seq,))] * 2
        + [dma((n_dp,))] * 2
        + [dma((2,))] * 2
        + [dma((chips,))] * 8
        + [dma((2,))] * 4
        + [dma((n_dp,))] * 2
        + [dma((2,))] * 2
        + [dma((10,))],
        compiler_params=pltpu.CompilerParams(
            collective_id=0, has_side_effects=True, vmem_limit_bytes=60 << 20
        ),
        name="backward",
    )(
        hidden, queries, keys, upstream, w_value, segment_ids, response_lengths,
        advantages, move_plan.T,
    )


def solution(mesh):
    placed = (
        P("dp", "seq", None),
        P("dp", "seq", None),
        P("dp", "seq", None),
        P("dp", "seq", None),
        P(("dp", "seq"), None),
        P("dp", "seq"),
        P("dp", None),
        P("dp", None),
        P(),
    )
    return jax.shard_map(
        on_device,
        mesh=mesh,
        in_specs=placed,
        out_specs=(P("dp", "seq", None), P(("dp", "seq"), None)),
        check_vma=False,
    )
```

time: 142 us -> 133 us (0.937)
  Pallas kernels: 136 us -> 128 us
    pallas_call x1, Pallas kernels: 136 us -> 128 us  [on_device(): pl.pallas_call(functools.partial(kernel, n_dp, n_seq), out_shape=(jax.Sha...]
where the time goes in v3:
time: 133 us; the launch traced here: 132 us
  Pallas kernels  128 us (96%)
  local copies, waits for them, and re-layouts  2.94 us (2%)
    pallas_call x1, Pallas kernels, on_device(): pl.pallas_call(functools.partial(kernel, n_dp, n_seq), out_shape=(jax.Sha...  128 us
    unnamed x2, local copies, waits for them, and re-layouts  2.94 us

profile of v3, /device:TPU:1, one launch (start us, length us, event | category | flops | bytes accessed | tf_op | source)
XLA Modules:
  0.0 132.0 jit_solution(1387408129174082222)
XLA Ops:
  0.6 128.4 %backward.1 = (bf16[2,64,512]{2,1,0:T(8,128)(2,1)}, f32[16,512]{1,0:T(8,128)}) custom-call(bf16[2,64,8192]{2,1,0:T(8,128)(2,1)} %hidden.1, bf16[2,64,4096]{2,1,0:T(8,128)(2,1)} %queries.1, bf16[2,64,512]{2,1,0:T(8,128)(2,1)} %keys.1, bf16[2,64,4096]{2,1,0:T(8,128)(2,1)} %upstream.1, bf16[16,512]{1,0:T(8,128)(2,1)} %w_value.1, s32[2,64]{1,0:T(2,128)} %segs.1, ...), custom_call_target="tpu_custom_call" | custom-call | tf_op jit(solution)/shard_map/backward/pallas_call | solution.py:516
  129.1 1.6 %copy.13 = bf16[2,64,512]{2,1,0:T(8,128)(2,1)} copy(bf16[2,64,512]{2,1,0:T(8,128)(2,1)} %get-tuple-element.4) | data formatting | bytes 262144
  130.6 1.4 %copy.14 = f32[16,512]{1,0:T(8,128)} copy(f32[16,512]{1,0:T(8,128)} %get-tuple-element.5) | data formatting | bytes 65536

commit v4 on v3

--- a/solution.py
+++ b/solution.py
@@ -88,13 +88,13 @@
 def kernel(
     n_dp, n_seq, hidden, queries, keys, upstream, w_value, segs, lengths, gains, plan,
     key_out, weight_out,
-    rows_in, perm, y, x, wg, seg, q, u, k, v, probs,
+    rows_in, perm, y, x, w_pair, wg, seg, q, u, k, v, probs,
     part, other, red, rs, dv_sum, dv_give, dv_got, vg, dk_sum, dk_own,
     kgs, kg, give, got, dw_far, dw_came, dw_near, dw_own, dw_got,
     s_send, s_recv, k_send, k_recv, q_send, q_recv, u_send, u_recv, o_send, o_recv, x_send, x_recv,
     w_send, w_recv, e_send, e_recv, p_send, p_recv, r_send, r_recv, a_send, a_recv, f_send, f_recv,
     t_send, t_recv, y_send, y_recv, z_send, z_recv,
-    c_send, c_recv, local,
+    c_send, c_recv, local, b_send, b_recv,
 ):
     rank, place = lax.axis_index("dp"), lax.axis_index("seq")
     rows = queries.shape[1]
@@ -108,6 +108,7 @@
     slot, head = chip // KVH, lax.rem(chip, KVH)
     depth = w_value.shape[0]
     n_z = n_dp // 2
+    width, columns = depth * n_dp, w_value.shape[1]
     lane, side = lax.rem(rank, n_z), rank // n_z
     f32, bf16 = jnp.float32, jnp.bfloat16
     scale = HD ** (-0.5)
@@ -145,9 +146,12 @@
         peer = lax.rem(place + m, n_seq)
         return remote(head_part(upstream, peer), u.at[aligned(place, rows)], u_send.at[m], u_recv.at[m], rank, peer)
 
+    def b_copy(n):
+        return remote(w_value, w_pair.at[side], b_send.at[n], b_recv.at[n], lane + n_z * (1 - side), place)
+
     def w_copy(m):
-        peer = lax.rem(rank + m, n_dp)
-        return remote(w_value, wg.at[aligned(rank, depth)], w_send.at[m], w_recv.at[m], peer, place)
+        peer = lax.rem(lane + m, n_z) + n_z * side
+        return remote(w_pair, wg.at[:, lane], w_send.at[m], w_recv.at[m], peer, place)
 
     def x_copy(m):
         peer = lax.rem(place + m, n_seq)
@@ -160,7 +164,7 @@
         pltpu.make_async_copy(k_part(place), k.at[aligned(place, rows)], local.at[2]),
         pltpu.make_async_copy(head_part(queries, place), q.at[aligned(place, rows)], local.at[3]),
         pltpu.make_async_copy(head_part(upstream, place), u.at[aligned(place, rows)], local.at[4]),
-        pltpu.make_async_copy(w_value, wg.at[aligned(rank, depth)], local.at[5]),
+        pltpu.make_async_copy(w_value, w_pair.at[side], local.at[5]),
     ]
 
     def send_keys():
@@ -173,8 +177,10 @@
     def send_upstream():
         copies.start("u", 1, n_seq, u_copy)
 
+    own_w = pltpu.make_async_copy(w_pair, wg.at[:, lane], local.at[10])
+
     def send_weights():
-        copies.start("w", 1, n_dp, w_copy)
+        copies.start("b", 0, 1, b_copy)
         for copy in own:
             copy.start()
 
@@ -215,6 +221,9 @@
                         ]
         for copy in own:
             copy.wait()
+        copies.arrive("b")
+        copies.start("w", 1, n_z, w_copy)
+        own_w.start()
 
     def send_hidden(n):
         copies.start(("x", n), n * n_seq + 1, (n + 1) * n_seq, x_copy)
@@ -304,7 +313,7 @@
         copies.landed.add("a")
 
     def project(n, which):
-        part[n, which] = jnp.dot(x[n, aligned(which, half), :], wg[...], preferred_element_type=f32).astype(bf16)
+        part[n, which] = jnp.dot(x[n, aligned(which, half), :], wg[...].reshape(width, columns), preferred_element_type=f32).astype(bf16)
 
     def e_copy(n):
         return remote(part.at[n, 1 - core], other.at[n], e_send.at[n], e_recv.at[n], rank, sibling)
@@ -312,6 +321,7 @@
     def project_values(n):
         if n == 0:
             copies.arrive("w")
+            own_w.wait()
         own_x[n].wait()
         copies.arrive(("x", n))
         project(n, 1 - core)
@@ -469,20 +479,20 @@
                 total = total + dw_got[m].astype(f32)
             weight_out[:, c * piece : (c + 1) * piece] = total
 
+    send_weights()
     send_keys()
     send_queries()
     send_upstream()
-    send_weights()
     regroup()
     send_hidden(0)
     make_probs()
     make_value_grads()
+    send_value_grads()
     project_values(0)
-    send_value_grads()
     project_values(1)
+    send_partials()
     forward_value_grads()
-    send_partials()
-    copies.settle("s", "k", "p", "q", "u", "w", ("x", 0), ("x", 1), ("e", 0), ("e", 1))
+    copies.settle("s", "k", "p", "q", "u", "b", "w", ("x", 0), ("x", 1), ("e", 0), ("e", 1))
     make_weight_grads()
     sum_values()
     send_weight_grads()
@@ -493,6 +503,11 @@
     end_trade()
     sum_weight_grads()
     copies.finish()
+
+
+def hand_over(key_ref, weight_ref, key_out, weight_out):
+    key_out[...] = key_ref[...]
+    weight_out[...] = weight_ref[...]
 
 
 def on_device(
@@ -513,7 +528,7 @@
     tiles = length // TILE
     triangle = TILE * tiles * (tiles + 1) // 2
     dma = pltpu.SemaphoreType.DMA
-    return pl.pallas_call(
+    key_grads, weight_grads = pl.pallas_call(
         functools.partial(kernel, n_dp, n_seq),
         out_shape=(
             jax.ShapeDtypeStruct((slots, rows, columns), bf16),
@@ -526,7 +541,8 @@
             pltpu.VMEM((square, square), bf16),
             pltpu.VMEM((slots, n_seq, rows, width), bf16),
             pltpu.VMEM((slots, length, width), bf16),
-            pltpu.VMEM((width, columns), bf16),
+            pltpu.VMEM((2, depth, columns), bf16),
+            pltpu.VMEM((2, n_dp // 2, depth, columns), bf16),
             pltpu.VMEM((n_seq, slots, rows), jnp.int32),
             pltpu.VMEM((length, wide), bf16),
             pltpu.VMEM((length, wide), bf16),
@@ -560,7 +576,7 @@
         + [dma((2,))] * 4
         + [dma((n_dp,))] * 2
         + [dma((2,))] * 2
-        + [dma((10,))],
+        + [dma((11,))] + [dma((1,))] * 2,
         compiler_params=pltpu.CompilerParams(
             collective_id=0, has_side_effects=True, vmem_limit_bytes=60 << 20
         ),
@@ -569,6 +585,16 @@
         hidden, queries, keys, upstream, w_value, segment_ids, response_lengths,
         advantages, move_plan.T,
     )
+    return pl.pallas_call(
+        hand_over,
+        out_shape=(
+            jax.ShapeDtypeStruct(key_grads.shape, key_grads.dtype),
+            jax.ShapeDtypeStruct(weight_grads.shape, weight_grads.dtype),
+        ),
+        in_specs=[VMEM, VMEM],
+        out_specs=[VMEM, VMEM],
+        name="hand_over",
+    )(key_grads, weight_grads)
 
 
 def solution(mesh):

time: 133 us -> 126 us (0.947)
  Pallas kernels: 128 us -> 125 us
  local copies, waits for them, and re-layouts: 2.94 us -> 0 us
    pallas_call x1, Pallas kernels: 128 us -> 124 us  [on_device(): pl.pallas_call(functools.partial(kernel, n_dp, n_seq), out_shape=(jax.Sha...]
    unnamed x2 -> x0, local copies, waits for them, and re-layouts: 2.94 us -> none
    pallas_call x0 -> x1, Pallas kernels: none -> 1.57 us  [on_device(): pl.pallas_call(hand_over, out_shape=(jax.ShapeDtypeStruct(key_grads.shape...]
where the time goes in v4:
time: 126 us
  Pallas kernels  125 us (99%)
    pallas_call x1, Pallas kernels, on_device(): pl.pallas_call(functools.partial(kernel, n_dp, n_seq), out_shape=(jax.Sha...  124 us

profile of v4, /device:TPU:1, one launch (start us, length us, event | category | flops | bytes accessed | tf_op | source)
XLA Modules:
  0.0 126.1 jit_solution(15636958166199391133)
XLA Ops:
  0.6 123.9 %backward.1 = (bf16[2,64,512]{2,1,0:T(8,128)(2,1)}, f32[16,512]{1,0:T(8,128)}) custom-call(bf16[2,64,8192]{2,1,0:T(8,128)(2,1)} %hidden.1, bf16[2,64,4096]{2,1,0:T(8,128)(2,1)} %queries.1, bf16[2,64,512]{2,1,0:T(8,128)(2,1)} %keys.1, bf16[2,64,4096]{2,1,0:T(8,128)(2,1)} %upstream.1, bf16[16,512]{1,0:T(8,128)(2,1)} %w_value.1, s32[2,64]{1,0:T(2,128)} %segs.1, ...), custom_call_target="tpu_custom_call" | custom-call | tf_op jit(solution)/shard_map/backward/pallas_call | solution.py:531
  124.5 1.6 %hand_over.1 = (bf16[2,64,512]{2,1,0:T(8,128)(2,1)}, f32[16,512]{1,0:T(8,128)}) custom-call(bf16[2,64,512]{2,1,0:T(8,128)(2,1)} %get-tuple-element.4.key_ref, f32[16,512]{1,0:T(8,128)} %get-tuple-element.5.weight_ref), custom_call_target="tpu_custom_call" | custom-call | tf_op jit(solution)/shard_map/hand_over/pallas_call | solution.py:588

commit v5 on v4

--- a/solution.py
+++ b/solution.py
@@ -240,7 +240,6 @@
             copies.arrive(name)
             if name == "k":
                 copies.start("p", 0, chips, k_pass)
-        send_hidden(1)
         copies.arrive("p")
         cut = find_cut()
 
@@ -485,6 +484,7 @@
     send_upstream()
     regroup()
     send_hidden(0)
+    send_hidden(1)
     make_probs()
     make_value_grads()
     send_value_grads()
@@ -534,7 +534,7 @@
             jax.ShapeDtypeStruct((slots, rows, columns), bf16),
             jax.ShapeDtypeStruct((depth, columns), f32),
         ),
-        in_specs=[ANY, ANY, ANY, ANY, VMEM, VMEM, SMEM, VMEM, SMEM],
+        in_specs=[ANY, ANY, ANY, ANY, ANY, ANY, SMEM, VMEM, SMEM],
         out_specs=[VMEM, VMEM],
         scratch_shapes=[
             pltpu.VMEM((slots, rows, features), bf16),

time: 126 us -> 126 us (level)
  no operation moved by 1% of the time
where the time goes in v5:
time: 126 us
  Pallas kernels  125 us (99%)
    pallas_call x1, Pallas kernels, on_device(): pl.pallas_call(functools.partial(kernel, n_dp, n_seq), out_shape=(jax.Sha...  123 us

profile of v5, /device:TPU:1, one launch (start us, length us, event | category | flops | bytes accessed | tf_op | source)
XLA Modules:
  0.0 125.7 jit_solution(1400103271572493920)
XLA Ops:
  0.6 123.5 %backward.1 = (bf16[2,64,512]{2,1,0:T(8,128)(2,1)}, f32[16,512]{1,0:T(8,128)}) custom-call(bf16[2,64,8192]{2,1,0:T(8,128)(2,1)} %hidden.1, bf16[2,64,4096]{2,1,0:T(8,128)(2,1)} %queries.1, bf16[2,64,512]{2,1,0:T(8,128)(2,1)} %keys.1, bf16[2,64,4096]{2,1,0:T(8,128)(2,1)} %upstream.1, bf16[16,512]{1,0:T(8,128)(2,1)} %w_value.1, s32[2,64]{1,0:T(2,128)} %segs.1, ...), custom_call_target="tpu_custom_call" | custom-call | tf_op jit(solution)/shard_map/backward/pallas_call | solution.py:531
  124.1 1.6 %hand_over.1 = (bf16[2,64,512]{2,1,0:T(8,128)(2,1)}, f32[16,512]{1,0:T(8,128)}) custom-call(bf16[2,64,512]{2,1,0:T(8,128)(2,1)} %get-tuple-element.4.key_ref, f32[16,512]{1,0:T(8,128)} %get-tuple-element.5.weight_ref), custom_call_target="tpu_custom_call" | custom-call | tf_op jit(solution)/shard_map/hand_over/pallas_call | solution.py:588
